TPU v7x, 128 devices: a whole 4x4x4 slice. The times are simulated.
128 devices in a mesh: row: 32 (over y_lo, x, z), col: 4 (over y_hi, core).
Axes of the slice: x: 4, y: 4 (y_hi: 2, y_lo: 2; y = y_hi * 2 + y_lo), z: 4, core: 2. Of those that a mesh axis runs over, the one named last changes fastest.
Arguments:
- old_basis: float32 [12288, 12288], P('row', 'col'), may hold values from -0.0546875 to 0.0546875
- updated_eigen_matrix: float32 [12288, 12288], P('row', 'col'), may hold values from -0.0546875 to 0.0546875
- moment: float32 [12288, 1536], P(('col', 'row')), may hold values from -6 to 6
Outputs:
- moment_in_new_frame: float32 [12288, 1536], P(('col', 'row'))
All inputs are finite; a program needn't handle non-finite values.
Results may differ from a plain program's by a relative error of at most 0.00008.
Values sent between devices are 32-bit elements; how exact they have to be, the bound alone decides.
A program may use at most 128 MiB of HBM per device.

v0:
```python
import jax
import jax.numpy as jnp
from jax import lax
from jax.sharding import PartitionSpec as P


def leftward_product(eigen_matrix_slice, right_factor):
    return lax.dot_general(
        eigen_matrix_slice,
        right_factor,
        (((0,), (0,)), ((), ())),
        precision=lax.Precision.HIGHEST,
        preferred_element_type=jnp.float32,
    )


def per_device(old_basis, updated_eigen_matrix, moment):
    collected_pieces = lax.all_gather(moment, "row", axis=0, tiled=True)
    partial_rows = jnp.dot(
        old_basis,
        collected_pieces,
        preferred_element_type=jnp.float32,
        precision=lax.Precision.HIGHEST,
    )
    standard_frame_moment = lax.psum(partial_rows, "col")
    return lax.psum_scatter(
        leftward_product(updated_eigen_matrix, standard_frame_moment),
        "row",
        scatter_dimension=0,
        tiled=True,
    )


def solution(mesh):
    placed = (P("row", "col"), P("row", "col"), P(("col", "row"), None))
    return jax.shard_map(
        per_device, mesh=mesh, in_specs=placed, out_specs=P(("col", "row"), None), check_vma=False
    )
```

profile of v0, /device:TPU:1, one launch (start us, length us, event | category | flops | bytes accessed | tf_op | source)
XLA Modules:
  0.0 585.2 jit_solution(3878502957933014729)
XLA Ops:
  6.5 0.0 all-gather.2.cloned.1.call-start
  6.5 0.7 all-gather.2.cloned.1.call-update
  7.3 0.0 all-reduce.2.cloned.1.call-start
  7.3 217.5 %all-gather.2.cloned.1.call-done = f32[3072,1536]{1,0:T(8,128)} async-done(((f32[96,1536]{1,0:T(8,128)}), f32[3072,1536]{1,0:T(8,128)}) %all-gather.2.cloned.1.call-update) | async-done | bytes 18874384 | tf_op jit(solution)/shard_map/all_gather | solution.py:18
  224.8 28.0 %fusion = f32[384,1536]{1,0:T(8,128)} fusion(f32[384,3072]{1,0:T(8,128)} %param.3, f32[3072,1536]{1,0:T(8,128)} %all-gather.2.cloned.1.call-done), kind=kOutput, calls=%fused_computation.1 | convolution fusion | flops 21743271936 | bytes 25952256 | tf_op jit(solution)/shard_map/dot_general | solution.py:19
  252.7 0.0 all-reduce.2.cloned.1.call-update
  252.7 0.2 reduce-scatter.4.cloned.1.call-start
  253.0 61.0 %all-reduce.2.cloned.1.call-done = f32[384,1536]{1,0:T(8,128)} async-done(((f32[384,1536]{1,0:T(8,128)}), f32[384,1536]{1,0:T(8,128)}) %all-reduce.2.cloned.1.call-update) | async-done | bytes 2359312 | tf_op jit(solution)/shard_map/psum | solution.py:25
  314.0 34.8 %convolution_bitcast_fusion = f32[3072,1536]{0,1:T(8,128)} fusion(f32[384,1536]{1,0:T(8,128)} %all-reduce.2.cloned.1.call-done, f32[384,3072]{1,0:T(8,128)} %param.4), kind=kOutput, calls=%fused_computation | convolution fusion | flops 21743271936 | bytes 25952256 | tf_op jit(solution)/shard_map/dot_general | solution.py:8
  348.7 18.7 %copy.6 = f32[3072,1536]{1,0:T(8,128)} copy(f32[3072,1536]{0,1:T(8,128)} %convolution_bitcast_fusion) | data formatting | bytes 37748736
  367.5 0.0 reduce-scatter.4.cloned.1.call-update
  367.5 211.2 %reduce-scatter.4.cloned.1.call-done = f32[96,1536]{1,0:T(8,128)} async-done(((f32[3072,1536]{1,0:T(8,128)}), f32[96,1536]{1,0:T(8,128)}) %reduce-scatter.4.cloned.1.call-update) | async-done | bytes 589840 | tf_op jit(solution)/shard_map/reduce_scatter | solution.py:26
Async XLA Ops:
  6.5 218.2 %all-gather.2.cloned.1.call-start = ((), (), s32[]{:S(2)}) async-start(), calls=%async_computation.1 | async-start | bytes 19464192 | tf_op jit(solution)/shard_map/all_gather | solution.py:18
  7.3 306.7 %all-reduce.2.cloned.1.call-start = ((), (), s32[]{:S(2)}) async-start(), calls=%async_computation.2 | async-start | bytes 4718592 | tf_op jit(solution)/shard_map/psum | solution.py:25
  252.7 326.0 %reduce-scatter.4.cloned.1.call-start = ((), (), s32[]{:S(2)}) async-start(), calls=%async_computation.3 | async-start | bytes 19464192 | tf_op jit(solution)/shard_map/reduce_scatter | solution.py:26
Sparse Core Ops, SparseCore 0:
  9.0 215.7 all-gather.1
  252.9 61.0 all-reduce.1
  367.6 211.0 reduce-scatter.3
where the time goes:
time: 589 us; the launch traced here: 585 us
  waiting for transfers between devices  490 us (83%)
  matrix products  62.7 us (11%)
  local copies, waits for them, and re-layouts  18.7 us (3%)
  between operations  13.1 us (2%)
    all_gather x1, waiting for transfers between devices, per_device(): collected_pieces = lax.all_gather(moment, 'row', axis=0, tiled=True)  217 us
    reduce_scatter x1, waiting for transfers between devices, per_device(): lax.psum_scatter(leftward_product(updated_eigen_matrix, standard_frame_mo...  211 us
    psum x1, waiting for transfers between devices, per_device(): standard_frame_moment = lax.psum(partial_rows, 'col')  61 us
    dot_general x1, matrix products, leftward_product(): lax.dot_general(eigen_matrix_slice, right_factor, (((0,), (0,)), ((), ())...  34.8 us
    dot_general x1, matrix products, per_device(): jnp.dot(old_basis, collected_pieces, preferred_element_type=jnp.float32,...  28 us
    unnamed x1, local copies, waits for them, and re-layouts  18.7 us
  transfers between devices with their start and end apart: 3, of which 3 were waited for; matrix products, arithmetic and copies ran while one was open for 0% of the time, Pallas kernels for 0%

commit v1 on v0

v1 whole, which is shorter than its diff:
```python
import functools

import jax
import jax.numpy as jnp
from jax import lax
from jax.experimental import pallas as pl
from jax.experimental.pallas import tpu as pltpu
from jax.sharding import PartitionSpec as P

ROWS, DEPTH, SLAB, PART = 384, 3072, 1536, 96
PLANE = DEPTH // 2
NCH = 3
CH = SLAB // NCH
HW = CH // 2
SLOTS = 2
MESH = pl.DeviceIdType.MESH
F32, BF16 = jnp.float32, jnp.bfloat16


def split(v):
    hi = v.astype(BF16)
    return hi, (v - hi.astype(F32)).astype(BF16)


def kernel(q_hbm, u_hbm, m_hbm, out, mg, qs, uts, urecv, stage, prod, rd, y1, rf, sf, shl, ob, v1, v2, w1, w2,
           ag_s, ag_r, rs_s, rs_r, ar_s, ar_r, pre_s, pre_r, own_sem, u_s, u_r, st_sem):
    row, col = lax.axis_index("row"), lax.axis_index("col")
    ylo, x, z = row // 16, lax.rem(row // 4, 4), lax.rem(row, 4)
    yhi, core = col // 2, lax.rem(col, 2)

    def plus(v, n):
        return lax.rem(v + n, 4)

    def in_plane(xx, zz):
        return (ylo * 16 + xx * 4 + zz, col)

    xp, xm = in_plane(plus(x, 1), z), in_plane(plus(x, 3), z)
    zp, zm = in_plane(x, plus(z, 1)), in_plane(x, plus(z, 3))
    pair = ((1 - ylo) * 16 + x * 4 + z, col)
    far = (row, (1 - yhi) * 2 + core)
    sib = (row, yhi * 2 + 1 - core)

    first = ((x, xp, xm), (z, zp, zm))
    second = ((z, zp, zm), (x, xp, xm))

    def block(h, a, b):
        xx, zz = (a, b) if h == 0 else (b, a)
        return pl.ds(pl.multiple_of(xx * 384 + zz * 96, 32), PART)

    def remote(src, dst, ss, rs, to):
        return pltpu.make_async_remote_copy(src_ref=src, dst_ref=dst, send_sem=ss, recv_sem=rs, device_id=to, device_id_type=MESH)

    sends = {}

    def send(key, src, dst, ss, rs, to):
        sends[key] = lambda: remote(src, dst, ss, rs, to)
        sends[key]().start()

    def landed(dst, ss, rs):
        remote(dst, dst, ss, rs, pair).wait_recv()

    def sent(key):
        sends.pop(key)().wait_send()

    barrier = pltpu.get_barrier_semaphore()
    for other in (xp, xm, zp, zm, pair, far, sib):
        pl.semaphore_signal(barrier, inc=1, device_id=other, device_id_type=MESH)
    pl.semaphore_wait(barrier, 7)

    own_rows = block(0, x, z)

    def columns(j, h):
        return pl.ds(j * CH + h * HW, HW)

    def own_copy(j, h):
        return pltpu.make_async_copy(m_hbm.at[:, columns(j, h)], mg.at[j, h, ylo, own_rows], own_sem.at[j, h])

    for j in range(NCH):
        for h in range(2):
            own_copy(j, h).start()
            send(("pre", j, h), m_hbm.at[:, columns(j, h)], mg.at[j, h, ylo, own_rows], pre_s.at[j, h], pre_r.at[j, h], pair)
    send(("u",), u_hbm.at[:, pl.ds(pl.multiple_of((1 - ylo) * PLANE, 128), PLANE)], urecv, u_s, u_r, pair)

    def load(i):
        if i < 4:
            src = q_hbm.at[:, pl.ds(i * 768, 768)]
        else:
            src = u_hbm.at[:, pl.ds(pl.multiple_of(ylo * PLANE + (i - 4) * 768, 128), 768)]
        return pltpu.make_async_copy(src, stage.at[i % 2], st_sem.at[i % 2])

    def turn(src, depth0, base):
        @pl.loop(0, 6)
        def _(i):
            at = pl.multiple_of(i * 128, 128)
            hi, lo = split(src[:, pl.ds(at, 128)].T)
            seg, r0 = base // 384 + i // 3, pl.multiple_of(lax.rem(i, 3) * 128, 128)
            uts[seg, pl.ds(r0, 128), pl.ds(depth0, 384)] = hi
            uts[seg, pl.ds(r0 + 384, 128), pl.ds(depth0, 384)] = lo

    def prepare(i):
        load(i).wait()
        if i < 4:
            @pl.loop(0, 24)
            def _(r):
                r0 = pl.multiple_of(r * 16, 16)
                hi, lo = split(stage[i % 2, pl.ds(r0, 16), :])
                qs[pl.ds(r0, 16), pl.ds(i * 768, 768)] = hi
                qs[pl.ds(r0 + 384, 16), pl.ds(i * 768, 768)] = lo
        else:
            turn(stage.at[i % 2], pl.multiple_of(ylo * 384, 128), (i - 4) * 768)
        if i + 2 < 6:
            load(i + 2).start()

    load(0).start()
    load(1).start()

    def prepare_received():
        landed(urecv, u_s, u_r)
        for i in range(2):
            turn(urecv.at[:, pl.ds(i * 768, 768)], pl.multiple_of((1 - ylo) * 384, 128), i * 768)

    def piece(j, h, a, b):
        return mg.at[j, h, :, block(h, a, b)]

    def pass_on(j, h, i, a, b, to):
        ref = piece(j, h, a, b)
        send(("ag", j, h, i), ref, ref, ag_s.at[j, h, i], ag_r.at[j, h, i], to)

    def arrived(j, h, i, a, b):
        landed(piece(j, h, a, b), ag_s.at[j, h, i], ag_r.at[j, h, i])

    def half_piece(j, h, part, a, b):
        return mg.at[j, h, part, block(h, a, b)]

    def ag0(j, h):
        (a, ap, am), (b, bp, bm) = first[h], second[h]
        own_copy(j, h).wait()
        landed(mg.at[j, h, 1 - ylo, own_rows], pre_s.at[j, h], pre_r.at[j, h])
        pass_on(j, h, 0, a, b, ap)
        pass_on(j, h, 1, a, b, am)
        pass_on(j, h, 4, a, b, bp)
        pass_on(j, h, 8, a, b, bm)

    def ag1(j, h):
        (a, ap, am), (b, bp, bm) = first[h], second[h]
        for i, rel, part, to in ((0, 3, 0, ap), (1, 1, 1, am)):
            arrived(j, h, i, plus(a, rel), b)
            ref = half_piece(j, h, part, plus(a, rel), b)
            send(("ag", j, h, 2 + part), ref, ref, ag_s.at[j, h, 2 + part], ag_r.at[j, h, 2 + part], to)
            pass_on(j, h, 4 + rel, plus(a, rel), b, bp)
            pass_on(j, h, 8 + rel, plus(a, rel), b, bm)

    def ag2(j, h):
        (a, ap, am), (b, bp, bm) = first[h], second[h]
        for part in range(2):
            landed(half_piece(j, h, part, plus(a, 2), b), ag_s.at[j, h, 2 + part], ag_r.at[j, h, 2 + part])
        pass_on(j, h, 6, plus(a, 2), b, bp)
        pass_on(j, h, 10, plus(a, 2), b, bm)

    def ag3(j, h, rel):
        (a, ap, am), (b, bp, bm) = first[h], second[h]
        aa = plus(a, rel)
        arrived(j, h, 4 + rel, aa, plus(b, 3))
        if rel < 2:
            pass_on(j, h, 12 + rel, aa, plus(b, 3), bp)
        arrived(j, h, 8 + rel, aa, plus(b, 1))
        if rel >= 2:
            pass_on(j, h, 12 + rel, aa, plus(b, 1), bm)

    def ag4(j, h):
        (a, ap, am), (b, bp, bm) = first[h], second[h]
        for rel in range(4):
            arrived(j, h, 12 + rel, plus(a, rel), plus(b, 2))

    def product1(j):
        @pl.loop(0, 2)
        def _(h):
            prod[j, h] = jnp.zeros((ROWS, HW), F32)

            @pl.loop(0, 4)
            def _(i):
                hi, lo = split(mg[j, h, i // 2, pl.ds(pl.multiple_of(lax.rem(i, 2) * 768, 768), 768), :])
                at = pl.ds(pl.multiple_of(i * 768, 128), 768)
                both = jnp.dot(qs[:, at], hi, preferred_element_type=F32)
                rest = jnp.dot(qs[pl.ds(0, 384), at], lo, preferred_element_type=F32)
                prod[j, h] += both[:ROWS] + (both[ROWS:] + rest)

        send(("ar", j, 0), prod.at[j, :, pl.ds(pl.multiple_of((1 - core) * 192, 192), 192)], rd.at[j], ar_s.at[j, 0], ar_r.at[j, 0], sib)

    def sum1(j):
        landed(rd.at[j], ar_s.at[j, 0], ar_r.at[j, 0])
        y1[j] = prod[j, :, pl.ds(pl.multiple_of(core * 192, 192), 192), :] + rd[j]
        send(("ar", j, 1), y1.at[j], rf.at[j], ar_s.at[j, 1], ar_r.at[j, 1], far)

    def sum2(j):
        landed(rf.at[j], ar_s.at[j, 1], ar_r.at[j, 1])
        sf[j, ylo, core] = y1[j] + rf[j]
        ref = sf.at[j, ylo, core]
        send(("ar", j, 2), ref, ref, ar_s.at[j, 2], ar_r.at[j, 2], pair)
        send(("ar", j, 3), ref, ref, ar_s.at[j, 3], ar_r.at[j, 3], sib)

    def sum3(j):
        ref = sf.at[j, 1 - ylo, core]
        landed(ref, ar_s.at[j, 2], ar_r.at[j, 2])
        send(("ar", j, 4), ref, ref, ar_s.at[j, 4], ar_r.at[j, 4], sib)

    def product2(j):
        landed(sf.at[j, ylo, 1 - core], ar_s.at[j, 3], ar_r.at[j, 3])
        landed(sf.at[j, 1 - ylo, 1 - core], ar_s.at[j, 4], ar_r.at[j, 4])
        slot = j % SLOTS
        if j >= SLOTS:
            for h in range(2):
                for i in range(16):
                    sent(("rs", j - SLOTS, h, i))

        @pl.loop(0, 2)
        def _(h):
            @pl.loop(0, 4)
            def _(i):
                hi, lo = split(sf[j, i // 2, lax.rem(i, 2), h])
                at = pl.ds(pl.multiple_of(i * 192, 192), 192)
                shl[0, at, :] = hi
                shl[1, at, :] = lo

            @pl.loop(0, 4)
            def _(seg):
                both = jnp.dot(uts[seg], shl[0], preferred_element_type=F32)
                rest = jnp.dot(uts[seg, pl.ds(0, 384), :], shl[1], preferred_element_type=F32)
                ob[slot, h, pl.ds(pl.multiple_of(seg * 384, 384), 384), :] = both[:384] + (both[384:] + rest)

    def o(j, h, a, b):
        return ob.at[j % SLOTS, h, block(h, a, b)]

    def rs_send(j, h, i, src, dst, to):
        send(("rs", j, h, i), src, dst, rs_s.at[j, h, i], rs_r.at[j, h, i], to)

    def rs_landed(j, h, i, dst):
        landed(dst, rs_s.at[j, h, i], rs_r.at[j, h, i])

    def rs0(j, h):
        (a, ap, am), (b, bp, bm) = first[h], second[h]
        for rel in (0, 2, 1, 3):
            rs_send(j, h, rel, o(j, h, plus(a, rel), plus(b, 2)), v1.at[j, h, rel], bp if rel < 2 else bm)
        for rel in (2, 0, 3, 1):
            if rel >= 2:
                rs_send(j, h, 4 + rel, o(j, h, plus(a, rel), plus(b, 1)), v2.at[j, h, 0, rel], bp)
            else:
                rs_send(j, h, 8 + rel, o(j, h, plus(a, rel), plus(b, 3)), v2.at[j, h, 1, rel], bm)

    def rs1(j, h):
        (a, ap, am), (b, bp, bm) = first[h], second[h]
        for rel in (0, 2, 1, 3):
            rs_landed(j, h, rel, v1.at[j, h, rel])
            ref = o(j, h, plus(a, rel), plus(b, 1 if rel < 2 else 3))
            ref[...] += v1[j, h, rel]
            if rel < 2:
                rs_send(j, h, 4 + rel, ref, v2.at[j, h, 0, rel], bp)
            else:
                rs_send(j, h, 8 + rel, ref, v2.at[j, h, 1, rel], bm)

    def rs2(j, h):
        (a, ap, am), (b, bp, bm) = first[h], second[h]
        for rel in (2, 1, 3, 0):
            for d in range(2):
                rs_landed(j, h, 4 + 4 * d + rel, v2.at[j, h, d, rel])
            ref = o(j, h, plus(a, rel), b)
            ref[...] += v2[j, h, 0, rel] + v2[j, h, 1, rel]
            if rel == 2:
                rs_send(j, h, 12, ref.at[pl.ds(0, 48)], w1.at[j, h, 0], ap)
                rs_send(j, h, 13, ref.at[pl.ds(48, 48)], w1.at[j, h, 1], am)

    def rs3(j, h):
        (a, ap, am), (b, bp, bm) = first[h], second[h]
        for d, rel, to in ((0, 1, ap), (1, 3, am)):
            rs_landed(j, h, 12 + d, w1.at[j, h, d])
            ref = o(j, h, plus(a, rel), b)
            ref[pl.ds(48 * d, 48), :] += w1[j, h, d]
            rs_send(j, h, 14 + d, ref, w2.at[j, h, d], to)

    def rs4(j, h):
        (a, ap, am), (b, bp, bm) = first[h], second[h]
        for d in range(2):
            rs_landed(j, h, 14 + d, w2.at[j, h, d])
        out[:, columns(j, h)] = o(j, h, a, b)[...] + (w2[j, h, 0] + w2[j, h, 1])

    steps = []

    def at(time, what):
        steps.append((time, len(steps), what))

    period = 94.0 / NCH
    for i in range(4):
        at(1.0 + i * 0.1, functools.partial(prepare, i))
    for i in range(4, 6):
        at(period * 0.6 + i * 0.1, functools.partial(prepare, i))
    at(period + 15.0, prepare_received)
    for j in range(NCH):
        t = period * j
        for h in range(2):
            at(t - 0.25 * period, functools.partial(ag0, j, h))
            at(t + 0.25 * period, functools.partial(ag1, j, h))
            at(t + 0.35 * period, functools.partial(ag3, j, h, 0))
            at(t + 0.50 * period, functools.partial(ag2, j, h))
            at(t + 0.64 * period, functools.partial(ag3, j, h, 1))
            at(t + 0.66 * period, functools.partial(ag3, j, h, 3))
            at(t + 0.80 * period, functools.partial(ag3, j, h, 2))
            at(t + 1.0 * period, functools.partial(ag4, j, h))
        e = t + period
        at(e + 0.5, functools.partial(product1, j))
        at(e + 5.0, functools.partial(sum1, j))
        at(e + 5.0 + 0.25 * period, functools.partial(sum2, j))
        at(e + 6.0 + 0.45 * period, functools.partial(sum3, j))
        e = e + 8.0 + 0.45 * period
        at(e, functools.partial(product2, j))
        for h in range(2):
            at(e + 0.1, functools.partial(rs0, j, h))
            at(e + 0.1 + 0.25 * period, functools.partial(rs1, j, h))
            at(e + 0.1 + 0.60 * period, functools.partial(rs2, j, h))
            at(e + 2.0 + 0.70 * period, functools.partial(rs3, j, h))
            at(e + 4.0 + 0.80 * period, functools.partial(rs4, j, h))
    for _, _, what in sorted(steps, key=lambda s: s[:2]):
        what()
    for key in list(sends):
        sent(key)


def per_device(old_basis, updated_eigen_matrix, moment):
    dma = pltpu.SemaphoreType.DMA
    return pl.pallas_call(
        kernel,
        out_shape=jax.ShapeDtypeStruct((PART, SLAB), F32),
        in_specs=[pl.BlockSpec(memory_space=pl.ANY)] * 3,
        out_specs=pl.BlockSpec(memory_space=pltpu.VMEM),
        scratch_shapes=[
            pltpu.VMEM((NCH, 2, 2, PLANE, HW), F32),
            pltpu.VMEM((2 * ROWS, DEPTH), BF16),
            pltpu.VMEM((4, 768, 768), BF16),
            pltpu.VMEM((ROWS, PLANE), F32),
            pltpu.VMEM((2, ROWS, 768), F32),
            pltpu.VMEM((NCH, 2, ROWS, HW), F32),
            pltpu.VMEM((NCH, 2, 192, HW), F32),
            pltpu.VMEM((NCH, 2, 192, HW), F32),
            pltpu.VMEM((NCH, 2, 192, HW), F32),
            pltpu.VMEM((NCH, 2, 2, 2, 192, HW), F32),
            pltpu.VMEM((2, 768, HW), BF16),
            pltpu.VMEM((SLOTS, 2, PLANE, HW), F32),
            pltpu.VMEM((NCH, 2, 4, PART, HW), F32),
            pltpu.VMEM((NCH, 2, 2, 4, PART, HW), F32),
            pltpu.VMEM((NCH, 2, 2, 48, HW), F32),
            pltpu.VMEM((NCH, 2, 2, PART, HW), F32),
            dma((NCH, 2, 16)), dma((NCH, 2, 16)), dma((NCH, 2, 16)), dma((NCH, 2, 16)),
            dma((NCH, 5)), dma((NCH, 5)), dma((NCH, 2)), dma((NCH, 2)), dma((NCH, 2)), dma(()), dma(()), dma((2,)),
        ],
        compiler_params=pltpu.CompilerParams(collective_id=0, has_side_effects=True, vmem_limit_bytes=63 * 2**20),
        cost_estimate=pl.CostEstimate(flops=21_700_000_000, bytes_accessed=10_000_000, transcendentals=0),
        name="rebase",
    )(old_basis, updated_eigen_matrix, moment)


def solution(mesh):
    placed = (P("row", "col"), P("row", "col"), P(("col", "row"), None))
    return jax.shard_map(
        per_device, mesh=mesh, in_specs=placed, out_specs=P(("col", "row"), None), check_vma=False
    )
```

time: 589 us -> 230 us (0.39)
  waiting for transfers between devices: 490 us -> 0 us
  Pallas kernels: 0 us -> 228 us
  matrix products: 62.7 us -> 0 us
  local copies, waits for them, and re-layouts: 18.7 us -> 1.92 us
  between operations: 13.1 us -> 0.01 us
    pallas_call x0 -> x1, Pallas kernels: none -> 228 us  [per_device(): pl.pallas_call(kernel, out_shape=jax.ShapeDtypeStruct((PART, SLAB), F32),...]
    all_gather x1 -> x0, waiting for transfers between devices: 217 us -> none  [per_device(): collected_pieces = lax.all_gather(moment, 'row', axis=0, tiled=True)]
    reduce_scatter x1 -> x0, waiting for transfers between devices: 211 us -> none  [per_device(): lax.psum_scatter(leftward_product(updated_eigen_matrix, standard_frame_mo...]
    dot_general x2 -> x0, matrix products: 62.7 us -> none  [the longest x1 34.8 us: leftward_product(): lax.dot_general(eigen_matrix_slice, right_factor, (((0,), (0,)), ((), ())...]
    psum x1 -> x0, waiting for transfers between devices: 61 us -> none  [per_device(): standard_frame_moment = lax.psum(partial_rows, 'col')]
    unnamed x1, local copies, waits for them, and re-layouts: 18.7 us -> 1.92 us
  transfers between devices with their start and end apart: 3 -> 0, of which waited for: 3 -> 0; matrix products, arithmetic and copies ran while one was open for 0% -> 0% of each run, Pallas kernels for 0% -> 0%
where the time goes in v1:
time: 230 us
  Pallas kernels  228 us (99%)
    pallas_call x1, Pallas kernels, per_device(): pl.pallas_call(kernel, out_shape=jax.ShapeDtypeStruct((PART, SLAB), F32),...  228 us

profile of v1, /device:TPU:1, one launch (start us, length us, event | category | flops | bytes accessed | tf_op | source)
XLA Modules:
  0.0 229.6 jit_solution(7844997489552775805)
XLA Ops:
  0.0 227.6 %rebase.1 = f32[96,1536]{1,0:T(8,128)} custom-call(f32[384,3072]{1,0:T(8,128)} %q_hbm.1, f32[384,3072]{1,0:T(8,128)} %u_hbm.1, f32[96,1536]{1,0:T(8,128)} %m_hbm.1), custom_call_target="tpu_custom_call" | custom-call | flops 21699999744 | bytes 10000000 | tf_op jit(solution)/shard_map/rebase/pallas_call | solution.py:329
  227.6 1.9 copy.5

commit v2 on v0

v2 whole, which is shorter than its diff:
```python
import jax
import jax.numpy as jnp
from jax import lax
from jax.experimental import pallas as pl
from jax.experimental.pallas import tpu as pltpu
from jax.sharding import PartitionSpec as P

ROWS, DEPTH, SLAB, PART = 384, 3072, 1536, 96
PLANE = DEPTH // 2
WIDTHS = (128, 256, 256, 128)
NCH = len(WIDTHS)
FROM = [2 * sum(WIDTHS[:j]) for j in range(NCH)]
ORDER = (
    ("hop", 0), ("prepare", 0), ("prepare", 1), ("prepare", 2), ("prepare", 3), ("ag0", 0, 0), ("ag0", 0, 1),
    ("hop", 1), ("prepare", 4), ("prepare", 5), ("hop", 2), ("hop", 3), ("ag1", 0, 0), ("ag1", 0, 1), ("exchange", 0),
    ("ag0", 1, 0), ("ag0", 1, 1), ("ag2", 0, 0), ("ag2", 0, 1), ("ag0", 2, 0), ("ag0", 2, 1), ("ag1", 1, 0),
    ("ag1", 1, 1), ("ag3", 0, 1), ("ag3", 0, 0), ("ag1", 2, 0), ("take", 0), ("exchange", 1), ("ag1", 2, 1),
    ("ag2", 1, 0), ("ag0", 3, 0), ("ag2", 1, 1), ("ag0", 3, 1), ("ag4", 0, 1), ("product1", 0, 1), ("ag4", 0, 0),
    ("product1", 0, 0), ("sum1", 0, 1), ("ag2", 2, 0), ("ag2", 2, 1), ("ag1", 3, 0), ("sum1", 0, 0), ("take", 1),
    ("exchange", 2), ("sum2", 0, 1), ("sum2", 0, 0), ("ag3", 1, 0), ("ag3", 1, 1), ("ag1", 3, 1), ("take", 2),
    ("exchange", 3), ("sum3", 0, 1), ("sum3", 0, 0), ("ag3", 2, 1), ("ag2", 3, 0), ("ag3", 2, 0), ("take", 3),
    ("product2", 0, 0), ("rs0", 0, 0), ("product2", 0, 1), ("ag4", 1, 0), ("ag4", 1, 1), ("product1", 1, 0),
    ("product1", 1, 1), ("sum1", 1, 0), ("ag2", 3, 1), ("rs0", 0, 1), ("sum1", 1, 1), ("ag4", 2, 1), ("product1", 2, 1),
    ("ag3", 3, 0), ("sum1", 2, 1), ("sum2", 1, 0), ("ag3", 3, 1), ("sum2", 1, 1), ("ag4", 2, 0), ("product1", 2, 0),
    ("rs1", 0, 0), ("sum2", 2, 1), ("rs1", 0, 1), ("sum1", 2, 0), ("sum3", 1, 0), ("ag4", 3, 1), ("product1", 3, 1),
    ("ag4", 3, 0), ("product1", 3, 0), ("sum1", 3, 1), ("rs2", 0, 1), ("product2", 1, 0), ("sum3", 1, 1),
    ("sum1", 3, 0), ("rs2", 0, 0), ("rs3", 0, 1), ("rs0", 1, 0), ("product2", 1, 1), ("sum3", 2, 1), ("rs3", 0, 0),
    ("rs4", 0, 1), ("rs0", 1, 1), ("product2", 2, 1), ("sum2", 2, 0), ("rs4", 0, 0), ("sum2", 3, 1), ("rs1", 1, 0),
    ("rs0", 2, 1), ("sum2", 3, 0), ("rs1", 1, 1), ("sum3", 2, 0), ("rs2", 1, 0), ("sum3", 3, 1), ("product2", 2, 0),
    ("sum3", 3, 0), ("rs0", 2, 0), ("rs1", 2, 1), ("product2", 3, 1), ("product2", 3, 0), ("rs0", 3, 0), ("rs0", 3, 1),
    ("rs1", 2, 0), ("rs2", 1, 1), ("rs3", 1, 0), ("rs1", 3, 0), ("rs2", 2, 1), ("rs1", 3, 1), ("rs2", 2, 0),
    ("rs4", 1, 0), ("rs3", 1, 1), ("rs2", 3, 1), ("rs2", 3, 0), ("rs3", 2, 0), ("rs3", 2, 1), ("rs4", 1, 1),
    ("rs3", 3, 0), ("rs3", 3, 1), ("rs4", 2, 0), ("rs4", 2, 1), ("rs4", 3, 0), ("rs4", 3, 1),
)
MESH = pl.DeviceIdType.MESH
F32, BF16 = jnp.float32, jnp.bfloat16


def split(v):
    hi = v.astype(BF16)
    return hi, (v - hi.astype(F32)).astype(BF16)


def kernel(q_hbm, u_hbm, m_hbm, out, *scratch):
    per_chunk, common = scratch[: 9 * NCH], scratch[9 * NCH :]
    mg, prod, rd, y1, rf, sf, v, w1, w2 = [per_chunk[i * NCH : (i + 1) * NCH] for i in range(9)]
    qs, uts, urecv, stage, shl, ag_s, ag_r, rs_s, rs_r, ar_s, ar_r, pre_s, pre_r, own_sem, u_s, u_r, st_sem = common
    row, col = lax.axis_index("row"), lax.axis_index("col")
    ylo, x, z = row // 16, lax.rem(row // 4, 4), lax.rem(row, 4)
    yhi, core = col // 2, lax.rem(col, 2)

    def plus(v, n):
        return lax.rem(v + n, 4)

    def in_plane(xx, zz):
        return (ylo * 16 + xx * 4 + zz, col)

    xp, xm = in_plane(plus(x, 1), z), in_plane(plus(x, 3), z)
    zp, zm = in_plane(x, plus(z, 1)), in_plane(x, plus(z, 3))
    pair = ((1 - ylo) * 16 + x * 4 + z, col)
    far = (row, (1 - yhi) * 2 + core)
    sib = (row, yhi * 2 + 1 - core)

    first = ((x, xp, xm), (z, zp, zm))
    second = ((z, zp, zm), (x, xp, xm))

    def remote(src, dst, ss, rs, to):
        return pltpu.make_async_remote_copy(src_ref=src, dst_ref=dst, send_sem=ss, recv_sem=rs, device_id=to, device_id_type=MESH)

    sends = {}

    pairs = {"ag": (ag_s, ag_r), "rs": (rs_s, rs_r), "ar": (ar_s, ar_r), "pre": (pre_s, pre_r), "u": (u_s, u_r)}

    def copy(key, src, dst, to):
        ss, rs = (sem.at[key[1:]] for sem in pairs[key[0]])
        return remote(src, dst, ss, rs, to)

    def send(key, src, dst, to):
        sends[key] = lambda: copy(key, src, dst, to)
        sends[key]().start()

    def landed(key, dst):
        copy(key, dst, dst, pair).wait_recv()

    def sent(key):
        sends.pop(key)().wait_send()

    barrier = pltpu.get_barrier_semaphore()
    for other in (xp, xm, zp, zm, pair, far, sib):
        pl.semaphore_signal(barrier, inc=1, device_id=other, device_id_type=MESH)
    pl.semaphore_wait(barrier, 7)

    def columns(j, h):
        return pl.ds(FROM[j] + h * WIDTHS[j], WIDTHS[j])

    def own_copy(j, h):
        return pltpu.make_async_copy(m_hbm.at[:, columns(j, h)], mg[j].at[h, ylo, x, z], own_sem.at[j, h])

    def hop(j):
        for h in range(2):
            own_copy(j, h).start()
            send(("pre", j, h), m_hbm.at[:, columns(j, h)], mg[j].at[h, ylo, x, z], pair)

    def exchange(i):
        at = pl.multiple_of((1 - ylo) * PLANE + 384 * i, 128)
        send(("u", i), u_hbm.at[:, pl.ds(at, 384)], urecv.at[i], pair)

    def load(i):
        if i < 4:
            src = q_hbm.at[:, pl.ds(i * 768, 768)]
        else:
            src = u_hbm.at[:, pl.ds(pl.multiple_of(ylo * PLANE + (i - 4) * 768, 128), 768)]
        return pltpu.make_async_copy(src, stage.at[i % 2], st_sem.at[i % 2])

    def turn(src, seg, depth0):
        @pl.loop(0, 3)
        def _(i):
            at = pl.multiple_of(i * 128, 128)
            hi, lo = split(src[:, pl.ds(at, 128)].T)
            uts[seg, pl.ds(at, 128), pl.ds(depth0, 384)] = hi
            uts[seg, pl.ds(at + 384, 128), pl.ds(depth0, 384)] = lo

    def prepare(i):
        load(i).wait()
        if i < 4:
            @pl.loop(0, 12)
            def _(r):
                r0 = pl.multiple_of(r * 32, 32)
                hi, lo = split(stage[i % 2, pl.ds(r0, 32), :])
                qs[pl.ds(r0, 32), pl.ds(i * 768, 768)] = hi
                qs[pl.ds(r0 + 384, 32), pl.ds(i * 768, 768)] = lo
        else:
            for half in range(2):
                turn(stage.at[i % 2, :, pl.ds(384 * half, 384)], 2 * (i - 4) + half, pl.multiple_of(ylo * 384, 128))
        if i + 2 < 6:
            load(i + 2).start()

    load(0).start()
    load(1).start()

    def take(i):
        landed(("u", i), urecv.at[i])
        turn(urecv.at[i], i, pl.multiple_of((1 - ylo) * 384, 128))

    def piece(j, h, a, b):
        return mg[j].at[h, :, a, b] if h == 0 else mg[j].at[h, :, b, a]

    def line(j, h, part, b):
        return mg[j].at[h, part, :, b] if h == 0 else mg[j].at[h, part, b]

    def lines(j, h, b):
        return mg[j].at[h, :, :, b] if h == 0 else mg[j].at[h, :, b]

    def half_piece(j, h, part, a, b):
        return mg[j].at[h, part, a, b] if h == 0 else mg[j].at[h, part, b, a]

    def pass_on(j, h, i, ref, to):
        send(("ag", j, h, i), ref, ref, to)

    def arrived(j, h, i, ref):
        landed(("ag", j, h, i), ref)

    def ag0(j, h):
        (a, ap, am), (b, bp, bm) = first[h], second[h]
        own_copy(j, h).wait()
        landed(("pre", j, h), mg[j].at[h, 1 - ylo, x, z])
        pass_on(j, h, 0, piece(j, h, a, b), ap)
        pass_on(j, h, 1, piece(j, h, a, b), am)

    def ag1(j, h):
        (a, ap, am), (b, bp, bm) = first[h], second[h]
        for i, rel, to in ((0, 3, ap), (1, 1, am)):
            arrived(j, h, i, piece(j, h, plus(a, rel), b))
            pass_on(j, h, 2 + i, half_piece(j, h, i, plus(a, rel), b), to)

    def ag2(j, h):
        (a, ap, am), (b, bp, bm) = first[h], second[h]
        for i in range(2):
            arrived(j, h, 2 + i, half_piece(j, h, i, plus(a, 2), b))
        pass_on(j, h, 4, lines(j, h, b), bp)
        pass_on(j, h, 5, lines(j, h, b), bm)

    def ag3(j, h):
        (a, ap, am), (b, bp, bm) = first[h], second[h]
        for i, rel, to in ((0, 3, bp), (1, 1, bm)):
            arrived(j, h, 4 + i, lines(j, h, plus(b, rel)))
            pass_on(j, h, 6 + i, line(j, h, i, plus(b, rel)), to)

    def ag4(j, h):
        (a, ap, am), (b, bp, bm) = first[h], second[h]
        for i in range(2):
            arrived(j, h, 6 + i, line(j, h, i, plus(b, 2)))

    def ar_send(j, h, i, src, dst, to):
        send(("ar", j, h, i), src, dst, to)

    def ar_landed(j, h, i, dst):
        landed(("ar", j, h, i), dst)

    def product1(j, h):
        prod[j][h] = jnp.zeros((ROWS, WIDTHS[j]), F32)

        @pl.loop(0, 4)
        def _(i):
            hi, lo = split(mg[j][h, i // 2, pl.ds(lax.rem(i, 2) * 2, 2)].reshape(768, WIDTHS[j]))
            at = pl.ds(pl.multiple_of(i * 768, 128), 768)
            both = jnp.dot(qs[:, at], hi, preferred_element_type=F32)
            rest = jnp.dot(qs[pl.ds(0, 384), at], lo, preferred_element_type=F32)
            prod[j][h] += both[:ROWS] + (both[ROWS:] + rest)

        ar_send(j, h, 0, prod[j].at[h, pl.ds(pl.multiple_of((1 - core) * 192, 192), 192)], rd[j].at[h], sib)

    def sum1(j, h):
        ar_landed(j, h, 0, rd[j].at[h])
        y1[j][h] = prod[j][h, pl.ds(pl.multiple_of(core * 192, 192), 192), :] + rd[j][h]
        ar_send(j, h, 1, y1[j].at[h], rf[j].at[h], far)

    def sum2(j, h):
        ar_landed(j, h, 1, rf[j].at[h])
        sf[j][h, ylo, core] = y1[j][h] + rf[j][h]
        ref = sf[j].at[h, ylo, core]
        ar_send(j, h, 2, ref, ref, pair)
        ar_send(j, h, 3, ref, ref, sib)

    def sum3(j, h):
        ref = sf[j].at[h, 1 - ylo, core]
        ar_landed(j, h, 2, ref)
        ar_send(j, h, 4, ref, ref, sib)

    def product2(j, h):
        w = WIDTHS[j]
        ar_landed(j, h, 3, sf[j].at[h, ylo, 1 - core])
        ar_landed(j, h, 4, sf[j].at[h, 1 - ylo, 1 - core])
        for i in range(8):
            sent(("ag", j, h, i))

        @pl.loop(0, 4)
        def _(i):
            hi, lo = split(sf[j][h, i // 2, lax.rem(i, 2)])
            at = pl.ds(pl.multiple_of(i * 192, 192), 192)
            shl[0, at, pl.ds(0, w)] = hi
            shl[1, at, pl.ds(0, w)] = lo

        @pl.loop(0, 4)
        def _(seg):
            both = jnp.dot(uts[seg], shl[0, :, pl.ds(0, w)], preferred_element_type=F32)
            rest = jnp.dot(uts[seg, pl.ds(0, 384), :], shl[1, :, pl.ds(0, w)], preferred_element_type=F32)
            mg[j][h, 0, seg] = (both[:384] + (both[384:] + rest)).reshape(4, PART, w)

    def o(j, h, a, b):
        return half_piece(j, h, 0, a, b)

    def rs_send(j, h, i, src, dst, to):
        send(("rs", j, h, i), src, dst, to)

    def rs_landed(j, h, i, dst):
        landed(("rs", j, h, i), dst)

    def rs0(j, h):
        (a, ap, am), (b, bp, bm) = first[h], second[h]
        for rel in (0, 2, 1, 3):
            rs_send(j, h, rel, o(j, h, plus(a, rel), plus(b, 2)), v[j].at[h, 0, rel], bp if rel < 2 else bm)
        for rel in (2, 0, 3, 1):
            if rel >= 2:
                rs_send(j, h, 4 + rel, o(j, h, plus(a, rel), plus(b, 1)), v[j].at[h, 1, rel], bp)
            else:
                rs_send(j, h, 8 + rel, o(j, h, plus(a, rel), plus(b, 3)), v[j].at[h, 2, rel], bm)

    def rs1(j, h):
        (a, ap, am), (b, bp, bm) = first[h], second[h]
        for rel in (0, 2, 1, 3):
            rs_landed(j, h, rel, v[j].at[h, 0, rel])
            ref = o(j, h, plus(a, rel), plus(b, 1 if rel < 2 else 3))
            ref[...] += v[j][h, 0, rel]
            if rel < 2:
                rs_send(j, h, 4 + rel, ref, v[j].at[h, 1, rel], bp)
            else:
                rs_send(j, h, 8 + rel, ref, v[j].at[h, 2, rel], bm)

    def rs2(j, h):
        (a, ap, am), (b, bp, bm) = first[h], second[h]
        for rel in (2, 1, 3, 0):
            for d in range(2):
                rs_landed(j, h, 4 + 4 * d + rel, v[j].at[h, 1 + d, rel])
            ref = o(j, h, plus(a, rel), b)
            ref[...] += v[j][h, 1, rel] + v[j][h, 2, rel]
            if rel == 2:
                rs_send(j, h, 12, ref.at[pl.ds(0, 48)], w1[j].at[h, 0], ap)
                rs_send(j, h, 13, ref.at[pl.ds(48, 48)], w1[j].at[h, 1], am)

    def rs3(j, h):
        (a, ap, am), (b, bp, bm) = first[h], second[h]
        for d, rel, to in ((0, 1, ap), (1, 3, am)):
            rs_landed(j, h, 12 + d, w1[j].at[h, d])
            ref = o(j, h, plus(a, rel), b)
            ref[pl.ds(48 * d, 48), :] += w1[j][h, d]
            rs_send(j, h, 14 + d, ref, w2[j].at[h, d], to)

    def rs4(j, h):
        (a, ap, am), (b, bp, bm) = first[h], second[h]
        for d in range(2):
            rs_landed(j, h, 14 + d, w2[j].at[h, d])
        out[:, columns(j, h)] = o(j, h, a, b)[...] + (w2[j][h, 0] + w2[j][h, 1])

    steps = dict(
        hop=hop, prepare=prepare, exchange=exchange, take=take, ag0=ag0, ag1=ag1, ag2=ag2, ag3=ag3, ag4=ag4,
        product1=product1, sum1=sum1, sum2=sum2, sum3=sum3, product2=product2, rs0=rs0, rs1=rs1, rs2=rs2, rs3=rs3, rs4=rs4,
    )
    for name, *where in ORDER:
        steps[name](*where)
    for key in list(sends):
        sent(key)


def per_device(old_basis, updated_eigen_matrix, moment):
    dma = pltpu.SemaphoreType.DMA
    shapes = ((2, 4, 4, PART), (ROWS,), (192,), (192,), (192,), (2, 2, 192), (3, 4, PART), (2, 48), (2, PART))
    return pl.pallas_call(
        kernel,
        out_shape=jax.ShapeDtypeStruct((PART, SLAB), F32),
        in_specs=[pl.BlockSpec(memory_space=pl.ANY)] * 3,
        out_specs=pl.BlockSpec(memory_space=pltpu.VMEM),
        scratch_shapes=[pltpu.VMEM((2, *shape, w), F32) for shape in shapes for w in WIDTHS] + [
            pltpu.VMEM((2 * ROWS, DEPTH), BF16),
            pltpu.VMEM((4, 768, 768), BF16),
            pltpu.VMEM((4, ROWS, 384), F32),
            pltpu.VMEM((2, ROWS, 768), F32),
            pltpu.VMEM((2, 768, max(WIDTHS)), BF16),
            dma((NCH, 2, 8)), dma((NCH, 2, 8)), dma((NCH, 2, 16)), dma((NCH, 2, 16)),
            dma((NCH, 2, 5)), dma((NCH, 2, 5)), dma((NCH, 2)), dma((NCH, 2)), dma((NCH, 2)), dma((4,)), dma((4,)), dma((2,)),
        ],
        compiler_params=pltpu.CompilerParams(collective_id=0, has_side_effects=True, vmem_limit_bytes=63 * 2**20),
        cost_estimate=pl.CostEstimate(flops=21_700_000_000, bytes_accessed=10_000_000, transcendentals=0),
        name="rebase",
    )(old_basis, updated_eigen_matrix, moment)


def solution(mesh):
    placed = (P("row", "col"), P("row", "col"), P(("col", "row"), None))
    return jax.shard_map(
        per_device, mesh=mesh, in_specs=placed, out_specs=P(("col", "row"), None), check_vma=False
    )
```

time: 589 us -> 180 us (0.31)
  waiting for transfers between devices: 490 us -> 0 us
  Pallas kernels: 0 us -> 178 us
  matrix products: 62.7 us -> 0 us
  local copies, waits for them, and re-layouts: 18.7 us -> 1.92 us
  between operations: 13.1 us -> 0.01 us
    all_gather x1 -> x0, waiting for transfers between devices: 217 us -> none  [per_device(): collected_pieces = lax.all_gather(moment, 'row', axis=0, tiled=True)]
    reduce_scatter x1 -> x0, waiting for transfers between devices: 211 us -> none  [per_device(): lax.psum_scatter(leftward_product(updated_eigen_matrix, standard_frame_mo...]
    pallas_call x0 -> x1, Pallas kernels: none -> 178 us  [per_device(): pl.pallas_call(kernel, out_shape=jax.ShapeDtypeStruct((PART, SLAB), F32),...]
    dot_general x2 -> x0, matrix products: 62.7 us -> none  [the longest x1 34.8 us: leftward_product(): lax.dot_general(eigen_matrix_slice, right_factor, (((0,), (0,)), ((), ())...]
    psum x1 -> x0, waiting for transfers between devices: 61 us -> none  [per_device(): standard_frame_moment = lax.psum(partial_rows, 'col')]
    unnamed x1, local copies, waits for them, and re-layouts: 18.7 us -> 1.92 us
  transfers between devices with their start and end apart: 3 -> 0, of which waited for: 3 -> 0; matrix products, arithmetic and copies ran while one was open for 0% -> 0% of each run, Pallas kernels for 0% -> 0%
where the time goes in v2:
time: 180 us; the launch traced here: 179 us
  Pallas kernels  178 us (99%)
  local copies, waits for them, and re-layouts  1.92 us (1%)
    pallas_call x1, Pallas kernels, per_device(): pl.pallas_call(kernel, out_shape=jax.ShapeDtypeStruct((PART, SLAB), F32),...  178 us

profile of v2, /device:TPU:1, one launch (start us, length us, event | category | flops | bytes accessed | tf_op | source)
XLA Modules:
  0.0 179.5 jit_solution(12955057439294902482)
XLA Ops:
  0.0 177.5 %rebase.1 = f32[96,1536]{1,0:T(8,128)} custom-call(f32[384,3072]{1,0:T(8,128)} %q_hbm.1, f32[384,3072]{1,0:T(8,128)} %u_hbm.1, f32[96,1536]{1,0:T(8,128)} %m_hbm.1), custom_call_target="tpu_custom_call" | custom-call | flops 21699999744 | bytes 10000000 | tf_op jit(solution)/shard_map/rebase/pallas_call | solution.py:318
  177.6 1.9 %copy.5 = f32[96,1536]{1,0:T(8,128)} copy(f32[96,1536]{1,0:T(8,128)} %rebase.1) | data formatting | bytes 1179648

commit v3 on v2

v3 whole, which is shorter than its diff:
```python
import jax
import jax.numpy as jnp
from jax import lax
from jax.experimental import pallas as pl
from jax.experimental.pallas import tpu as pltpu
from jax.sharding import PartitionSpec as P

ROWS, DEPTH, SLAB, PART = 384, 3072, 1536, 96
PLANE = DEPTH // 2
WIDTHS = (256, 128, 128, 128, 128)
NCH = len(WIDTHS)
FROM = [2 * sum(WIDTHS[:j]) for j in range(NCH)]
ORDER = (
    ("hop", 0), ("ag0", 0, 0), ("ag0", 0, 1), ("ag0", 1, 0), ("ag0", 1, 1), ("prepare", 0), ("prepare", 1),
    ("prepare", 2), ("prepare", 3), ("agx", 0, 0), ("agx", 0, 1), ("hop", 1), ("prepare", 4), ("prepare", 5),
    ("hop", 2), ("ag0", 2, 0), ("ag0", 2, 1), ("hop", 3), ("ag0", 3, 0), ("ag0", 3, 1), ("hop", 4), ("agx", 1, 0),
    ("ag1", 0, 0), ("ag1", 0, 1), ("agx", 1, 1), ("agx", 2, 0), ("agx", 2, 1), ("ag1", 1, 0), ("agx", 3, 0),
    ("ag2", 0, 1), ("agx", 3, 1), ("ag0", 4, 1), ("ag2", 0, 0), ("ag1", 1, 1), ("exchange", 0), ("exchange", 1),
    ("exchange", 2), ("exchange", 3), ("ag0", 4, 0), ("ag1", 2, 0), ("ag1", 2, 1), ("agx", 4, 0), ("agx", 4, 1),
    ("ag2", 1, 0), ("ag1", 3, 1), ("ag1", 3, 0), ("ag3", 0, 1), ("ag3", 0, 0), ("ag2", 1, 1), ("ag2", 2, 0),
    ("ag2", 2, 1), ("ag1", 4, 0), ("ag1", 4, 1), ("ag2", 3, 0), ("ag3", 1, 0), ("ag4", 0, 1), ("product1", 0, 1),
    ("ag2", 3, 1), ("sum1", 0, 1), ("ag3", 1, 1), ("ag4", 0, 0), ("product1", 0, 0), ("sum1", 0, 0), ("ag3", 2, 1),
    ("ag3", 2, 0), ("ag2", 4, 0), ("ag2", 4, 1), ("take", 0), ("take", 1), ("take", 2), ("take", 3), ("sum2", 0, 1),
    ("ag3", 3, 1), ("ag3", 3, 0), ("sum2", 0, 0), ("ag4", 1, 1), ("ag4", 1, 0), ("product1", 1, 0), ("sum3", 0, 1),
    ("ag4", 2, 1), ("ag4", 2, 0), ("sum1", 1, 0), ("product1", 2, 0), ("sum3", 0, 0), ("product2", 0, 1),
    ("sum1", 2, 0), ("product2", 0, 0), ("sum2", 1, 0), ("ag3", 4, 0), ("ag3", 4, 1), ("rs0", 0, 0), ("rs0", 0, 1),
    ("ag4", 3, 1), ("ag4", 3, 0), ("sum2", 2, 0), ("product1", 3, 0), ("sum3", 1, 0), ("ag4", 4, 1), ("ag4", 4, 0),
    ("product1", 4, 0), ("sum1", 3, 0), ("product2", 1, 0), ("sum3", 2, 0), ("sum1", 4, 0), ("rs1", 0, 0),
    ("rs1", 0, 1), ("rs0", 1, 0), ("rs0", 1, 1), ("product2", 2, 0), ("sum2", 3, 0), ("rs0", 2, 0), ("rs0", 2, 1),
    ("rs2", 0, 0), ("rs2", 0, 1), ("sum2", 4, 0), ("rs1", 1, 0), ("rs1", 1, 1), ("sum3", 3, 0), ("rs1", 2, 0),
    ("rs1", 2, 1), ("product2", 3, 0), ("sum3", 4, 0), ("rs3", 0, 0), ("rs3", 0, 1), ("rs0", 3, 0), ("rs0", 3, 1),
    ("rs2", 1, 0), ("rs2", 1, 1), ("product2", 4, 0), ("rs2", 2, 0), ("rs2", 2, 1), ("rs4", 0, 1), ("rs4", 0, 0),
    ("rs0", 4, 0), ("rs0", 4, 1), ("rs1", 3, 0), ("rs1", 3, 1), ("rs3", 1, 1), ("rs3", 1, 0), ("rs3", 2, 1),
    ("rs3", 2, 0), ("rs1", 4, 0), ("rs1", 4, 1), ("rs2", 3, 0), ("rs2", 3, 1), ("rs4", 1, 1), ("rs4", 1, 0),
    ("rs4", 2, 1), ("rs4", 2, 0), ("rs2", 4, 0), ("rs2", 4, 1), ("rs3", 3, 0), ("rs3", 3, 1), ("rs3", 4, 0),
    ("rs3", 4, 1), ("rs4", 3, 0), ("rs4", 3, 1), ("rs4", 4, 0), ("rs4", 4, 1),
)
MESH = pl.DeviceIdType.MESH
F32, BF16 = jnp.float32, jnp.bfloat16


def split(v):
    hi = v.astype(BF16)
    return hi, (v - hi.astype(F32)).astype(BF16)


def kernel(q_hbm, u_hbm, m_hbm, out, *scratch):
    per_chunk, common = scratch[: 9 * NCH], scratch[9 * NCH :]
    mg, prod, rd, y1, rf, sf, v, w1, w2 = [per_chunk[i * NCH : (i + 1) * NCH] for i in range(9)]
    qs, uts, urecv, stage, shl, ag_s, ag_r, rs_s, rs_r, ar_s, ar_r, pre_s, pre_r, own_sem, u_s, u_r, st_sem = common
    row, col = lax.axis_index("row"), lax.axis_index("col")
    ylo, x, z = row // 16, lax.rem(row // 4, 4), lax.rem(row, 4)
    yhi, core = col // 2, lax.rem(col, 2)

    def plus(v, n):
        return lax.rem(v + n, 4)

    def in_plane(xx, zz):
        return (ylo * 16 + xx * 4 + zz, col)

    xp, xm = in_plane(plus(x, 1), z), in_plane(plus(x, 3), z)
    zp, zm = in_plane(x, plus(z, 1)), in_plane(x, plus(z, 3))
    pair = ((1 - ylo) * 16 + x * 4 + z, col)
    far = (row, (1 - yhi) * 2 + core)
    sib = (row, yhi * 2 + 1 - core)

    first = ((x, xp, xm), (z, zp, zm))
    second = ((z, zp, zm), (x, xp, xm))

    def remote(src, dst, ss, rs, to):
        return pltpu.make_async_remote_copy(src_ref=src, dst_ref=dst, send_sem=ss, recv_sem=rs, device_id=to, device_id_type=MESH)

    sends = {}

    pairs = {"ag": (ag_s, ag_r), "rs": (rs_s, rs_r), "ar": (ar_s, ar_r), "pre": (pre_s, pre_r), "u": (u_s, u_r)}

    def copy(key, src, dst, to):
        ss, rs = (sem.at[key[1:]] for sem in pairs[key[0]])
        return remote(src, dst, ss, rs, to)

    def send(key, src, dst, to):
        sends[key] = lambda: copy(key, src, dst, to)
        sends[key]().start()

    def landed(key, dst):
        copy(key, dst, dst, pair).wait_recv()

    def sent(key):
        sends.pop(key)().wait_send()

    barrier = pltpu.get_barrier_semaphore()
    for other in (xp, xm, zp, zm, pair, far, sib):
        pl.semaphore_signal(barrier, inc=1, device_id=other, device_id_type=MESH)
    pl.semaphore_wait(barrier, 7)

    def columns(j, h):
        return pl.ds(FROM[j] + h * WIDTHS[j], WIDTHS[j])

    def own_piece(j, h, part):
        return mg[j].at[h, part, z, x] if h == 0 else mg[j].at[h, part, x, z]

    def own_copy(j, h):
        return pltpu.make_async_copy(m_hbm.at[:, columns(j, h)], own_piece(j, h, ylo), own_sem.at[j, h])

    def hop(j):
        for h in range(2):
            send(("pre", j, h), m_hbm.at[:, columns(j, h)], own_piece(j, h, ylo), pair)

    for j in range(NCH):
        for h in range(2):
            own_copy(j, h).start()

    def exchange(i):
        at = pl.multiple_of((1 - ylo) * PLANE + 384 * i, 128)
        send(("u", i), u_hbm.at[:, pl.ds(at, 384)], urecv.at[i], pair)

    def load(i):
        if i < 4:
            src = q_hbm.at[:, pl.ds(i * 768, 768)]
        else:
            src = u_hbm.at[:, pl.ds(pl.multiple_of(ylo * PLANE + (i - 4) * 768, 128), 768)]
        return pltpu.make_async_copy(src, stage.at[i % 2], st_sem.at[i % 2])

    def turn(src, seg, depth0):
        @pl.loop(0, 3)
        def _(i):
            at = pl.multiple_of(i * 128, 128)
            hi, lo = split(src[:, pl.ds(at, 128)].T)
            uts[seg, pl.ds(at, 128), pl.ds(depth0, 384)] = hi
            uts[seg, pl.ds(at + 384, 128), pl.ds(depth0, 384)] = lo

    def prepare(i):
        load(i).wait()
        if i < 4:
            @pl.loop(0, 12)
            def _(r):
                r0 = pl.multiple_of(r * 32, 32)
                hi, lo = split(stage[i % 2, pl.ds(r0, 32), :])
                qs[pl.ds(r0, 32), pl.ds(i * 768, 768)] = hi
                qs[pl.ds(r0 + 384, 32), pl.ds(i * 768, 768)] = lo
        else:
            for half in range(2):
                turn(stage.at[i % 2, :, pl.ds(384 * half, 384)], 2 * (i - 4) + half, pl.multiple_of(ylo * 384, 128))
        if i + 2 < 6:
            load(i + 2).start()

    load(0).start()
    load(1).start()

    def take(i):
        landed(("u", i), urecv.at[i])
        turn(urecv.at[i], i, pl.multiple_of((1 - ylo) * 384, 128))

    def piece(j, h, a, b):
        return mg[j].at[h, :, b, a]

    def line(j, h, part, b):
        return mg[j].at[h, part, b]

    def lines(j, h, b):
        return mg[j].at[h, :, b]

    def half_piece(j, h, part, a, b):
        return mg[j].at[h, part, b, a]

    def pass_on(j, h, i, ref, to):
        send(("ag", j, h, i), ref, ref, to)

    def arrived(j, h, i, ref):
        landed(("ag", j, h, i), ref)

    def ag0(j, h):
        (a, ap, am), (b, bp, bm) = first[h], second[h]
        own_copy(j, h).wait()
        pass_on(j, h, 0, half_piece(j, h, ylo, a, b), ap)
        pass_on(j, h, 1, half_piece(j, h, ylo, a, b), am)

    def agx(j, h):
        (a, ap, am), (b, bp, bm) = first[h], second[h]
        landed(("pre", j, h), own_piece(j, h, 1 - ylo))
        pass_on(j, h, 8, half_piece(j, h, 1 - ylo, a, b), ap)
        pass_on(j, h, 9, half_piece(j, h, 1 - ylo, a, b), am)

    def ag1(j, h):
        (a, ap, am), (b, bp, bm) = first[h], second[h]
        for i, rel, to in ((0, 3, ap), (1, 1, am)):
            arrived(j, h, i, half_piece(j, h, ylo, plus(a, rel), b))
            arrived(j, h, 8 + i, half_piece(j, h, 1 - ylo, plus(a, rel), b))
            pass_on(j, h, 2 + i, half_piece(j, h, i, plus(a, rel), b), to)

    def ag2(j, h):
        (a, ap, am), (b, bp, bm) = first[h], second[h]
        for i in range(2):
            arrived(j, h, 2 + i, half_piece(j, h, i, plus(a, 2), b))
        pass_on(j, h, 4, lines(j, h, b), bp)
        pass_on(j, h, 5, lines(j, h, b), bm)

    def ag3(j, h):
        (a, ap, am), (b, bp, bm) = first[h], second[h]
        for i, rel, to in ((0, 3, bp), (1, 1, bm)):
            arrived(j, h, 4 + i, lines(j, h, plus(b, rel)))
            pass_on(j, h, 6 + i, line(j, h, i, plus(b, rel)), to)

    def ag4(j, h):
        (a, ap, am), (b, bp, bm) = first[h], second[h]
        for i in range(2):
            arrived(j, h, 6 + i, line(j, h, i, plus(b, 2)))

    def halves(j, g):
        return ((0, 1), pl.ds(0, 2)) if WIDTHS[j] < 256 else ((g,), pl.ds(g, 1))

    def ar_send(j, g, i, src, dst, to):
        send(("ar", j, g, i), src, dst, to)

    def ar_landed(j, g, i, dst):
        landed(("ar", j, g, i), dst)

    def moment_rows(j, h, part, x0):
        if h == 0:
            return jnp.concatenate([mg[j][0, part, zz, x0 + xx] for xx in range(2) for zz in range(4)], axis=0)
        return mg[j][1, part, pl.ds(x0, 2)].reshape(768, WIDTHS[j])

    def product1(j, g):
        hs, sl = halves(j, g)
        w = WIDTHS[j]
        prod[j][sl] = jnp.zeros((len(hs), ROWS, w), F32)

        @pl.loop(0, 4)
        def _(i):
            rows = [moment_rows(j, h, i // 2, lax.rem(i, 2) * 2) for h in hs]
            hi, lo = split(jnp.concatenate(rows, axis=1) if len(hs) > 1 else rows[0])
            at = pl.ds(pl.multiple_of(i * 768, 128), 768)
            both = jnp.dot(qs[:, at], hi, preferred_element_type=F32)
            rest = jnp.dot(qs[pl.ds(0, 384), at], lo, preferred_element_type=F32)
            total = both[:ROWS] + (both[ROWS:] + rest)
            for n, h in enumerate(hs):
                prod[j][h] += total[:, n * w : (n + 1) * w]

        ar_send(j, g, 0, prod[j].at[sl, pl.ds(pl.multiple_of((1 - core) * 192, 192), 192)], rd[j].at[sl], sib)

    def sum1(j, g):
        hs, sl = halves(j, g)
        ar_landed(j, g, 0, rd[j].at[sl])
        y1[j][sl] = prod[j][sl, pl.ds(pl.multiple_of(core * 192, 192), 192), :] + rd[j][sl]
        ar_send(j, g, 1, y1[j].at[sl], rf[j].at[sl], far)

    def sum2(j, g):
        hs, sl = halves(j, g)
        ar_landed(j, g, 1, rf[j].at[sl])
        sf[j][sl, ylo, core] = y1[j][sl] + rf[j][sl]
        ref = sf[j].at[sl, ylo, core]
        ar_send(j, g, 2, ref, ref, pair)
        ar_send(j, g, 3, ref, ref, sib)

    def sum3(j, g):
        hs, sl = halves(j, g)
        ref = sf[j].at[sl, 1 - ylo, core]
        ar_landed(j, g, 2, ref)
        ar_send(j, g, 4, ref, ref, sib)

    def product2(j, g):
        hs, sl = halves(j, g)
        w = WIDTHS[j]
        ar_landed(j, g, 3, sf[j].at[sl, ylo, 1 - core])
        ar_landed(j, g, 4, sf[j].at[sl, 1 - ylo, 1 - core])
        for h in hs:
            for i in range(10):
                sent(("ag", j, h, i))

        @pl.loop(0, 4)
        def _(i):
            at = pl.ds(pl.multiple_of(i * 192, 192), 192)
            for n, h in enumerate(hs):
                hi, lo = split(sf[j][h, i // 2, lax.rem(i, 2)])
                shl[0, at, pl.ds(n * w, w)] = hi
                shl[1, at, pl.ds(n * w, w)] = lo

        @pl.loop(0, 4)
        def _(seg):
            both = jnp.dot(uts[seg], shl[0, :, pl.ds(0, len(hs) * w)], preferred_element_type=F32)
            rest = jnp.dot(uts[seg, pl.ds(0, 384), :], shl[1, :, pl.ds(0, len(hs) * w)], preferred_element_type=F32)
            total = both[:384] + (both[384:] + rest)
            for n, h in enumerate(hs):
                blocks = total[:, n * w : (n + 1) * w].reshape(4, PART, w)
                if h == 0:
                    mg[j][0, 0, :, seg] = blocks
                else:
                    mg[j][1, 0, seg] = blocks

    def o(j, h, a, b):
        return mg[j].at[h, 0, b, a]

    def half(k):
        return pl.ds(2 * k, 2)

    def o_half(j, h, k, b):
        return mg[j].at[h, 0, b, half(k)]

    def rs_send(j, h, i, src, dst, to):
        send(("rs", j, h, i), src, dst, to)

    def rs_landed(j, h, i, dst):
        landed(("rs", j, h, i), dst)

    def rs0(j, h):
        (a, ap, am), (b, bp, bm) = first[h], second[h]
        rs_send(j, h, 0, o_half(j, h, 0, plus(b, 2)), v[j].at[h, 0, half(0)], bp)
        rs_send(j, h, 1, o_half(j, h, 1, plus(b, 2)), v[j].at[h, 0, half(1)], bm)
        rs_send(j, h, 2, o_half(j, h, 1, plus(b, 1)), v[j].at[h, 1, half(1)], bp)
        rs_send(j, h, 3, o_half(j, h, 0, plus(b, 3)), v[j].at[h, 2, half(0)], bm)

    def rs1(j, h):
        (a, ap, am), (b, bp, bm) = first[h], second[h]
        for k, bb, to in ((0, plus(b, 1), bp), (1, plus(b, 3), bm)):
            rs_landed(j, h, k, v[j].at[h, 0, half(k)])
            ref = o_half(j, h, k, bb)
            ref[...] += v[j][h, 0, half(k)]
            rs_send(j, h, 4 + k, ref, v[j].at[h, 1 + k, half(k)], to)

    def rs2(j, h):
        (a, ap, am), (b, bp, bm) = first[h], second[h]
        rs_landed(j, h, 2, v[j].at[h, 1, half(1)])
        rs_landed(j, h, 3, v[j].at[h, 2, half(0)])
        rs_landed(j, h, 4, v[j].at[h, 1, half(0)])
        rs_landed(j, h, 5, v[j].at[h, 2, half(1)])
        ref = mg[j].at[h, 0, b]
        ref[...] += v[j][h, 1] + v[j][h, 2]
        far_block = o(j, h, plus(a, 2), b)
        rs_send(j, h, 6, far_block.at[pl.ds(0, 48)], w1[j].at[h, 0], ap)
        rs_send(j, h, 7, far_block.at[pl.ds(48, 48)], w1[j].at[h, 1], am)

    def rs3(j, h):
        (a, ap, am), (b, bp, bm) = first[h], second[h]
        for d, rel, to in ((0, 1, ap), (1, 3, am)):
            rs_landed(j, h, 6 + d, w1[j].at[h, d])
            ref = o(j, h, plus(a, rel), b)
            ref[pl.ds(48 * d, 48), :] += w1[j][h, d]
            rs_send(j, h, 8 + d, ref, w2[j].at[h, d], to)

    def rs4(j, h):
        (a, ap, am), (b, bp, bm) = first[h], second[h]
        for d in range(2):
            rs_landed(j, h, 8 + d, w2[j].at[h, d])
        out[:, columns(j, h)] = o(j, h, a, b)[...] + (w2[j][h, 0] + w2[j][h, 1])
        for key in [k for k in sends if k[1:3] == (j, h)]:
            sent(key)

    steps = dict(
        hop=hop, prepare=prepare, exchange=exchange, take=take, ag0=ag0, agx=agx, ag1=ag1, ag2=ag2, ag3=ag3, ag4=ag4,
        product1=product1, sum1=sum1, sum2=sum2, sum3=sum3, product2=product2, rs0=rs0, rs1=rs1, rs2=rs2, rs3=rs3, rs4=rs4,
    )
    for name, *where in ORDER:
        steps[name](*where)
    for key in list(sends):
        sent(key)


def per_device(old_basis, updated_eigen_matrix, moment):
    dma = pltpu.SemaphoreType.DMA
    shapes = ((2, 4, 4, PART), (ROWS,), (192,), (192,), (192,), (2, 2, 192), (3, 4, PART), (2, 48), (2, PART))
    return pl.pallas_call(
        kernel,
        out_shape=jax.ShapeDtypeStruct((PART, SLAB), F32),
        in_specs=[pl.BlockSpec(memory_space=pl.ANY)] * 3,
        out_specs=pl.BlockSpec(memory_space=pltpu.VMEM),
        scratch_shapes=[pltpu.VMEM((2, *shape, w), F32) for shape in shapes for w in WIDTHS] + [
            pltpu.VMEM((2 * ROWS, DEPTH), BF16),
            pltpu.VMEM((4, 768, 768), BF16),
            pltpu.VMEM((4, ROWS, 384), F32),
            pltpu.VMEM((2, ROWS, 768), F32),
            pltpu.VMEM((2, 768, 256), BF16),
            dma((NCH, 2, 10)), dma((NCH, 2, 10)), dma((NCH, 2, 10)), dma((NCH, 2, 10)),
            dma((NCH, 2, 5)), dma((NCH, 2, 5)), dma((NCH, 2)), dma((NCH, 2)), dma((NCH, 2)), dma((4,)), dma((4,)), dma((2,)),
        ],
        compiler_params=pltpu.CompilerParams(collective_id=0, has_side_effects=True, vmem_limit_bytes=63 * 2**20),
        cost_estimate=pl.CostEstimate(flops=21_700_000_000, bytes_accessed=10_000_000, transcendentals=0),
        name="rebase",
    )(old_basis, updated_eigen_matrix, moment)


def solution(mesh):
    placed = (P("row", "col"), P("row", "col"), P(("col", "row"), None))
    return jax.shard_map(
        per_device, mesh=mesh, in_specs=placed, out_specs=P(("col", "row"), None), check_vma=False
    )
```

time: 180 us -> 166 us (0.922)
  Pallas kernels: 178 us -> 162 us
    pallas_call x1, Pallas kernels: 178 us -> 162 us  [per_device(): pl.pallas_call(kernel, out_shape=jax.ShapeDtypeStruct((PART, SLAB), F32),...]
where the time goes in v3:
time: 166 us; the launch traced here: 164 us
  Pallas kernels  162 us (98%)
  local copies, waits for them, and re-layouts  1.92 us (1%)
    pallas_call x1, Pallas kernels, per_device(): pl.pallas_call(kernel, out_shape=jax.ShapeDtypeStruct((PART, SLAB), F32),...  162 us

profile of v3, /device:TPU:1, one launch (start us, length us, event | category | flops | bytes accessed | tf_op | source)
XLA Modules:
  0.0 164.0 jit_solution(3775368789310179965)
XLA Ops:
  0.0 162.0 %rebase.1 = f32[96,1536]{1,0:T(8,128)} custom-call(f32[384,3072]{1,0:T(8,128)} %q_hbm.1, f32[384,3072]{1,0:T(8,128)} %u_hbm.1, f32[96,1536]{1,0:T(8,128)} %m_hbm.1), custom_call_target="tpu_custom_call" | custom-call | flops 21699999744 | bytes 10000000 | tf_op jit(solution)/shard_map/rebase/pallas_call | solution.py:361
  162.0 1.9 %copy.5 = f32[96,1536]{1,0:T(8,128)} copy(f32[96,1536]{1,0:T(8,128)} %rebase.1) | data formatting | bytes 1179648

commit v4 on v3

--- a/solution.py
+++ b/solution.py
@@ -11,29 +11,29 @@
 NCH = len(WIDTHS)
 FROM = [2 * sum(WIDTHS[:j]) for j in range(NCH)]
 ORDER = (
-    ("hop", 0), ("ag0", 0, 0), ("ag0", 0, 1), ("ag0", 1, 0), ("ag0", 1, 1), ("prepare", 0), ("prepare", 1),
-    ("prepare", 2), ("prepare", 3), ("agx", 0, 0), ("agx", 0, 1), ("hop", 1), ("prepare", 4), ("prepare", 5),
-    ("hop", 2), ("ag0", 2, 0), ("ag0", 2, 1), ("hop", 3), ("ag0", 3, 0), ("ag0", 3, 1), ("hop", 4), ("agx", 1, 0),
-    ("ag1", 0, 0), ("ag1", 0, 1), ("agx", 1, 1), ("agx", 2, 0), ("agx", 2, 1), ("ag1", 1, 0), ("agx", 3, 0),
-    ("ag2", 0, 1), ("agx", 3, 1), ("ag0", 4, 1), ("ag2", 0, 0), ("ag1", 1, 1), ("exchange", 0), ("exchange", 1),
-    ("exchange", 2), ("exchange", 3), ("ag0", 4, 0), ("ag1", 2, 0), ("ag1", 2, 1), ("agx", 4, 0), ("agx", 4, 1),
-    ("ag2", 1, 0), ("ag1", 3, 1), ("ag1", 3, 0), ("ag3", 0, 1), ("ag3", 0, 0), ("ag2", 1, 1), ("ag2", 2, 0),
+    ("hop", 0), ("ag0", 0, 1), ("ag0", 1, 1), ("ag0", 0, 0), ("ag0", 1, 0), ("ag0", 2, 0), ("prepare", 0),
+    ("prepare", 1), ("prepare", 2), ("prepare", 3), ("agx", 0, 1), ("hop", 1), ("hop", 2), ("agx", 0, 0), ("hop", 3),
+    ("hop", 4), ("ag0", 2, 1), ("ag0", 3, 1), ("ag0", 3, 0), ("prepare", 4), ("prepare", 5), ("agx", 1, 0),
+    ("ag1", 0, 1), ("agx", 1, 1), ("ag1", 0, 0), ("agx", 2, 0), ("agx", 2, 1), ("ag1", 1, 0), ("agx", 3, 0),
+    ("ag2", 0, 1), ("ag0", 4, 1), ("agx", 3, 1), ("ag2", 0, 0), ("ag0", 4, 0), ("ag1", 1, 1), ("exchange", 0),
+    ("exchange", 1), ("exchange", 2), ("exchange", 3), ("ag1", 2, 0), ("ag1", 2, 1), ("agx", 4, 0), ("agx", 4, 1),
+    ("ag2", 1, 0), ("ag1", 3, 0), ("ag1", 3, 1), ("ag3", 0, 1), ("ag3", 0, 0), ("ag2", 1, 1), ("ag2", 2, 0),
     ("ag2", 2, 1), ("ag1", 4, 0), ("ag1", 4, 1), ("ag2", 3, 0), ("ag3", 1, 0), ("ag4", 0, 1), ("product1", 0, 1),
     ("ag2", 3, 1), ("sum1", 0, 1), ("ag3", 1, 1), ("ag4", 0, 0), ("product1", 0, 0), ("sum1", 0, 0), ("ag3", 2, 1),
     ("ag3", 2, 0), ("ag2", 4, 0), ("ag2", 4, 1), ("take", 0), ("take", 1), ("take", 2), ("take", 3), ("sum2", 0, 1),
     ("ag3", 3, 1), ("ag3", 3, 0), ("sum2", 0, 0), ("ag4", 1, 1), ("ag4", 1, 0), ("product1", 1, 0), ("sum3", 0, 1),
-    ("ag4", 2, 1), ("ag4", 2, 0), ("sum1", 1, 0), ("product1", 2, 0), ("sum3", 0, 0), ("product2", 0, 1),
-    ("sum1", 2, 0), ("product2", 0, 0), ("sum2", 1, 0), ("ag3", 4, 0), ("ag3", 4, 1), ("rs0", 0, 0), ("rs0", 0, 1),
-    ("ag4", 3, 1), ("ag4", 3, 0), ("sum2", 2, 0), ("product1", 3, 0), ("sum3", 1, 0), ("ag4", 4, 1), ("ag4", 4, 0),
-    ("product1", 4, 0), ("sum1", 3, 0), ("product2", 1, 0), ("sum3", 2, 0), ("sum1", 4, 0), ("rs1", 0, 0),
-    ("rs1", 0, 1), ("rs0", 1, 0), ("rs0", 1, 1), ("product2", 2, 0), ("sum2", 3, 0), ("rs0", 2, 0), ("rs0", 2, 1),
-    ("rs2", 0, 0), ("rs2", 0, 1), ("sum2", 4, 0), ("rs1", 1, 0), ("rs1", 1, 1), ("sum3", 3, 0), ("rs1", 2, 0),
-    ("rs1", 2, 1), ("product2", 3, 0), ("sum3", 4, 0), ("rs3", 0, 0), ("rs3", 0, 1), ("rs0", 3, 0), ("rs0", 3, 1),
-    ("rs2", 1, 0), ("rs2", 1, 1), ("product2", 4, 0), ("rs2", 2, 0), ("rs2", 2, 1), ("rs4", 0, 1), ("rs4", 0, 0),
-    ("rs0", 4, 0), ("rs0", 4, 1), ("rs1", 3, 0), ("rs1", 3, 1), ("rs3", 1, 1), ("rs3", 1, 0), ("rs3", 2, 1),
-    ("rs3", 2, 0), ("rs1", 4, 0), ("rs1", 4, 1), ("rs2", 3, 0), ("rs2", 3, 1), ("rs4", 1, 1), ("rs4", 1, 0),
-    ("rs4", 2, 1), ("rs4", 2, 0), ("rs2", 4, 0), ("rs2", 4, 1), ("rs3", 3, 0), ("rs3", 3, 1), ("rs3", 4, 0),
-    ("rs3", 4, 1), ("rs4", 3, 0), ("rs4", 3, 1), ("rs4", 4, 0), ("rs4", 4, 1),
+    ("ag4", 2, 1), ("ag4", 2, 0), ("product1", 2, 0), ("sum3", 0, 0), ("sum1", 1, 0), ("product2", 0, 1),
+    ("sum1", 2, 0), ("product2", 0, 0), ("ag3", 4, 1), ("ag3", 4, 0), ("rs0", 0, 1), ("rs0", 0, 0), ("sum2", 1, 0),
+    ("ag4", 3, 1), ("ag4", 3, 0), ("product1", 3, 0), ("sum2", 2, 0), ("ag4", 4, 1), ("ag4", 4, 0), ("sum1", 3, 0),
+    ("product1", 4, 0), ("sum3", 1, 0), ("rs1", 0, 1), ("rs1", 0, 0), ("sum1", 4, 0), ("product2", 1, 0), ("rs0", 1, 0),
+    ("sum3", 2, 0), ("rs0", 1, 1), ("sum2", 3, 0), ("product2", 2, 0), ("rs0", 2, 1), ("rs2", 0, 0), ("rs2", 0, 1),
+    ("sum2", 4, 0), ("rs0", 2, 0), ("rs1", 1, 0), ("rs1", 1, 1), ("sum3", 3, 0), ("rs3", 0, 1), ("rs1", 2, 1),
+    ("product2", 3, 0), ("sum3", 4, 0), ("rs0", 3, 1), ("rs3", 0, 0), ("rs0", 3, 0), ("rs1", 2, 0), ("product2", 4, 0),
+    ("rs0", 4, 0), ("rs0", 4, 1), ("rs2", 2, 1), ("rs4", 0, 1), ("rs1", 3, 1), ("rs1", 3, 0), ("rs2", 1, 1),
+    ("rs2", 1, 0), ("rs4", 0, 0), ("rs2", 2, 0), ("rs1", 4, 1), ("rs1", 4, 0), ("rs3", 2, 1), ("rs2", 3, 1),
+    ("rs3", 1, 0), ("rs2", 3, 0), ("rs3", 2, 0), ("rs3", 1, 1), ("rs2", 4, 1), ("rs2", 4, 0), ("rs4", 1, 0),
+    ("rs4", 2, 1), ("rs3", 3, 0), ("rs3", 3, 1), ("rs4", 2, 0), ("rs4", 1, 1), ("rs3", 4, 0), ("rs3", 4, 1),
+    ("rs4", 3, 0), ("rs4", 3, 1), ("rs4", 4, 0), ("rs4", 4, 1),
 )
 MESH = pl.DeviceIdType.MESH
 F32, BF16 = jnp.float32, jnp.bfloat16
@@ -88,11 +88,6 @@
     def sent(key):
         sends.pop(key)().wait_send()
 
-    barrier = pltpu.get_barrier_semaphore()
-    for other in (xp, xm, zp, zm, pair, far, sib):
-        pl.semaphore_signal(barrier, inc=1, device_id=other, device_id_type=MESH)
-    pl.semaphore_wait(barrier, 7)
-
     def columns(j, h):
         return pl.ds(FROM[j] + h * WIDTHS[j], WIDTHS[j])
 
@@ -105,10 +100,6 @@
     def hop(j):
         for h in range(2):
             send(("pre", j, h), m_hbm.at[:, columns(j, h)], own_piece(j, h, ylo), pair)
-
-    for j in range(NCH):
-        for h in range(2):
-            own_copy(j, h).start()
 
     def exchange(i):
         at = pl.multiple_of((1 - ylo) * PLANE + 384 * i, 128)
@@ -144,8 +135,16 @@
         if i + 2 < 6:
             load(i + 2).start()
 
+    for j in range(NCH):
+        for h in range(2):
+            own_copy(j, h).start()
     load(0).start()
     load(1).start()
+
+    barrier = pltpu.get_barrier_semaphore()
+    for other in (xp, xm, zp, zm, pair, far, sib):
+        pl.semaphore_signal(barrier, inc=1, device_id=other, device_id_type=MESH)
+    pl.semaphore_wait(barrier, 7)
 
     def take(i):
         landed(("u", i), urecv.at[i])

time: 166 us -> 164 us (0.988); the launches traced: 164 us -> 164 us
  no operation moved by 1% of the time
where the time goes in v4:
time: 164 us
  Pallas kernels  162 us (99%)
  local copies, waits for them, and re-layouts  1.92 us (1%)
    pallas_call x1, Pallas kernels, per_device(): pl.pallas_call(kernel, out_shape=jax.ShapeDtypeStruct((PART, SLAB), F32),...  162 us

profile of v4, /device:TPU:1, one launch (start us, length us, event | category | flops | bytes accessed | tf_op | source)
XLA Modules:
  0.0 164.1 jit_solution(16307618234006243667)
XLA Ops:
  0.0 162.2 %rebase.1 = f32[96,1536]{1,0:T(8,128)} custom-call(f32[384,3072]{1,0:T(8,128)} %q_hbm.1, f32[384,3072]{1,0:T(8,128)} %u_hbm.1, f32[96,1536]{1,0:T(8,128)} %m_hbm.1), custom_call_target="tpu_custom_call" | custom-call | flops 21699999744 | bytes 10000000 | tf_op jit(solution)/shard_map/rebase/pallas_call | solution.py:360
  162.2 1.9 %copy.5 = f32[96,1536]{1,0:T(8,128)} copy(f32[96,1536]{1,0:T(8,128)} %rebase.1) | data formatting | bytes 1179648

commit v5 on v4

--- a/solution.py
+++ b/solution.py
@@ -11,29 +11,29 @@
 NCH = len(WIDTHS)
 FROM = [2 * sum(WIDTHS[:j]) for j in range(NCH)]
 ORDER = (
-    ("hop", 0), ("ag0", 0, 1), ("ag0", 1, 1), ("ag0", 0, 0), ("ag0", 1, 0), ("ag0", 2, 0), ("prepare", 0),
-    ("prepare", 1), ("prepare", 2), ("prepare", 3), ("agx", 0, 1), ("hop", 1), ("hop", 2), ("agx", 0, 0), ("hop", 3),
-    ("hop", 4), ("ag0", 2, 1), ("ag0", 3, 1), ("ag0", 3, 0), ("prepare", 4), ("prepare", 5), ("agx", 1, 0),
-    ("ag1", 0, 1), ("agx", 1, 1), ("ag1", 0, 0), ("agx", 2, 0), ("agx", 2, 1), ("ag1", 1, 0), ("agx", 3, 0),
-    ("ag2", 0, 1), ("ag0", 4, 1), ("agx", 3, 1), ("ag2", 0, 0), ("ag0", 4, 0), ("ag1", 1, 1), ("exchange", 0),
-    ("exchange", 1), ("exchange", 2), ("exchange", 3), ("ag1", 2, 0), ("ag1", 2, 1), ("agx", 4, 0), ("agx", 4, 1),
-    ("ag2", 1, 0), ("ag1", 3, 0), ("ag1", 3, 1), ("ag3", 0, 1), ("ag3", 0, 0), ("ag2", 1, 1), ("ag2", 2, 0),
-    ("ag2", 2, 1), ("ag1", 4, 0), ("ag1", 4, 1), ("ag2", 3, 0), ("ag3", 1, 0), ("ag4", 0, 1), ("product1", 0, 1),
-    ("ag2", 3, 1), ("sum1", 0, 1), ("ag3", 1, 1), ("ag4", 0, 0), ("product1", 0, 0), ("sum1", 0, 0), ("ag3", 2, 1),
-    ("ag3", 2, 0), ("ag2", 4, 0), ("ag2", 4, 1), ("take", 0), ("take", 1), ("take", 2), ("take", 3), ("sum2", 0, 1),
-    ("ag3", 3, 1), ("ag3", 3, 0), ("sum2", 0, 0), ("ag4", 1, 1), ("ag4", 1, 0), ("product1", 1, 0), ("sum3", 0, 1),
-    ("ag4", 2, 1), ("ag4", 2, 0), ("product1", 2, 0), ("sum3", 0, 0), ("sum1", 1, 0), ("product2", 0, 1),
-    ("sum1", 2, 0), ("product2", 0, 0), ("ag3", 4, 1), ("ag3", 4, 0), ("rs0", 0, 1), ("rs0", 0, 0), ("sum2", 1, 0),
-    ("ag4", 3, 1), ("ag4", 3, 0), ("product1", 3, 0), ("sum2", 2, 0), ("ag4", 4, 1), ("ag4", 4, 0), ("sum1", 3, 0),
-    ("product1", 4, 0), ("sum3", 1, 0), ("rs1", 0, 1), ("rs1", 0, 0), ("sum1", 4, 0), ("product2", 1, 0), ("rs0", 1, 0),
-    ("sum3", 2, 0), ("rs0", 1, 1), ("sum2", 3, 0), ("product2", 2, 0), ("rs0", 2, 1), ("rs2", 0, 0), ("rs2", 0, 1),
-    ("sum2", 4, 0), ("rs0", 2, 0), ("rs1", 1, 0), ("rs1", 1, 1), ("sum3", 3, 0), ("rs3", 0, 1), ("rs1", 2, 1),
-    ("product2", 3, 0), ("sum3", 4, 0), ("rs0", 3, 1), ("rs3", 0, 0), ("rs0", 3, 0), ("rs1", 2, 0), ("product2", 4, 0),
-    ("rs0", 4, 0), ("rs0", 4, 1), ("rs2", 2, 1), ("rs4", 0, 1), ("rs1", 3, 1), ("rs1", 3, 0), ("rs2", 1, 1),
-    ("rs2", 1, 0), ("rs4", 0, 0), ("rs2", 2, 0), ("rs1", 4, 1), ("rs1", 4, 0), ("rs3", 2, 1), ("rs2", 3, 1),
-    ("rs3", 1, 0), ("rs2", 3, 0), ("rs3", 2, 0), ("rs3", 1, 1), ("rs2", 4, 1), ("rs2", 4, 0), ("rs4", 1, 0),
-    ("rs4", 2, 1), ("rs3", 3, 0), ("rs3", 3, 1), ("rs4", 2, 0), ("rs4", 1, 1), ("rs3", 4, 0), ("rs3", 4, 1),
-    ("rs4", 3, 0), ("rs4", 3, 1), ("rs4", 4, 0), ("rs4", 4, 1),
+    ("hop", 0), ("ag0", 0, 0), ("ag0", 0, 1), ("ag0", 1, 0), ("ag0", 1, 1), ("ag0", 2, 1), ("agx", 0, 0), ("ag0", 2, 0),
+    ("agx", 0, 1), ("hop", 1), ("ag0", 3, 0), ("ag0", 3, 1), ("ag0", 4, 0), ("hop", 2), ("ag1", 0, 0), ("hop", 3),
+    ("hop", 4), ("ag0", 4, 1), ("ag1", 0, 1), ("agx", 1, 0), ("agx", 2, 0), ("agx", 1, 1), ("exchange", 0),
+    ("agx", 2, 1), ("agx", 3, 0), ("ag2", 0, 0), ("ag1", 1, 0), ("agx", 4, 0), ("ag2", 0, 1), ("prepare", 0),
+    ("prepare", 1), ("prepare", 2), ("prepare", 3), ("ag1", 2, 1), ("ag1", 2, 0), ("ag1", 1, 1), ("agx", 3, 1),
+    ("agx", 4, 1), ("exchange", 1), ("ag3", 0, 0), ("ag1", 3, 0), ("exchange", 2), ("ag1", 4, 0), ("ag3", 0, 1),
+    ("ag2", 1, 0), ("exchange", 3), ("ag1", 3, 1), ("ag2", 1, 1), ("prepare", 4), ("prepare", 5), ("ag4", 0, 1),
+    ("ag2", 2, 0), ("product1", 0, 1), ("ag2", 2, 1), ("sum1", 0, 1), ("ag4", 0, 0), ("ag3", 1, 1), ("ag1", 4, 1),
+    ("ag3", 1, 0), ("product1", 0, 0), ("sum1", 0, 0), ("ag3", 2, 1), ("ag3", 2, 0), ("ag2", 3, 1), ("ag4", 1, 1),
+    ("ag2", 4, 1), ("ag2", 3, 0), ("ag4", 1, 0), ("ag2", 4, 0), ("take", 0), ("take", 1), ("take", 2), ("take", 3),
+    ("sum2", 0, 1), ("ag4", 2, 1), ("product1", 1, 0), ("sum2", 0, 0), ("ag4", 2, 0), ("product1", 2, 0),
+    ("sum3", 0, 1), ("sum1", 1, 0), ("ag3", 3, 0), ("ag3", 3, 1), ("sum1", 2, 0), ("sum3", 0, 0), ("product2", 0, 1),
+    ("product2", 0, 0), ("ag3", 4, 1), ("sum2", 1, 0), ("ag3", 4, 0), ("rs0", 0, 1), ("sum2", 2, 0), ("rs0", 0, 0),
+    ("ag4", 3, 1), ("ag4", 3, 0), ("product1", 3, 0), ("sum3", 1, 0), ("ag4", 4, 1), ("ag4", 4, 0), ("sum1", 3, 0),
+    ("product1", 4, 0), ("sum3", 2, 0), ("rs1", 0, 1), ("rs1", 0, 0), ("sum1", 4, 0), ("product2", 1, 0),
+    ("sum2", 3, 0), ("rs0", 1, 1), ("rs0", 1, 0), ("product2", 2, 0), ("rs0", 2, 1), ("sum2", 4, 0), ("rs0", 2, 0),
+    ("rs2", 0, 0), ("rs1", 1, 0), ("sum3", 3, 0), ("rs1", 1, 1), ("rs2", 0, 1), ("product2", 3, 0), ("rs0", 3, 1),
+    ("rs0", 3, 0), ("sum3", 4, 0), ("rs1", 2, 1), ("rs1", 2, 0), ("product2", 4, 0), ("rs0", 4, 1), ("rs0", 4, 0),
+    ("rs1", 3, 1), ("rs1", 3, 0), ("rs1", 4, 1), ("rs2", 1, 0), ("rs1", 4, 0), ("rs2", 2, 0), ("rs2", 2, 1),
+    ("rs3", 0, 0), ("rs2", 1, 1), ("rs2", 3, 1), ("rs2", 3, 0), ("rs3", 0, 1), ("rs2", 4, 1), ("rs2", 4, 0),
+    ("rs3", 1, 0), ("rs3", 2, 0), ("rs3", 2, 1), ("rs3", 1, 1), ("rs3", 3, 1), ("rs3", 3, 0), ("rs4", 0, 1),
+    ("rs3", 4, 0), ("rs3", 4, 1), ("rs4", 0, 0), ("rs4", 2, 1), ("rs4", 2, 0), ("rs4", 1, 0), ("rs4", 3, 0),
+    ("rs4", 1, 1), ("rs4", 3, 1), ("rs4", 4, 0), ("rs4", 4, 1),
 )
 MESH = pl.DeviceIdType.MESH
 F32, BF16 = jnp.float32, jnp.bfloat16

time: 164 us -> 160 us (0.976)
  Pallas kernels: 162 us -> 158 us
    pallas_call x1, Pallas kernels: 162 us -> 158 us  [per_device(): pl.pallas_call(kernel, out_shape=jax.ShapeDtypeStruct((PART, SLAB), F32),...]
where the time goes in v5:
time: 160 us
  Pallas kernels  158 us (99%)
  local copies, waits for them, and re-layouts  1.92 us (1%)
    pallas_call x1, Pallas kernels, per_device(): pl.pallas_call(kernel, out_shape=jax.ShapeDtypeStruct((PART, SLAB), F32),...  158 us

profile of v5, /device:TPU:1, one launch (start us, length us, event | category | flops | bytes accessed | tf_op | source)
XLA Modules:
  0.0 160.1 jit_solution(6850283920619716778)
XLA Ops:
  0.0 158.2 %rebase.1 = f32[96,1536]{1,0:T(8,128)} custom-call(f32[384,3072]{1,0:T(8,128)} %q_hbm.1, f32[384,3072]{1,0:T(8,128)} %u_hbm.1, f32[96,1536]{1,0:T(8,128)} %m_hbm.1), custom_call_target="tpu_custom_call" | custom-call | flops 21699999744 | bytes 10000000 | tf_op jit(solution)/shard_map/rebase/pallas_call | solution.py:360
  158.2 1.9 %copy.5 = f32[96,1536]{1,0:T(8,128)} copy(f32[96,1536]{1,0:T(8,128)} %rebase.1) | data formatting | bytes 1179648

commit v6 on v5

--- a/solution.py
+++ b/solution.py
@@ -7,33 +7,33 @@
 
 ROWS, DEPTH, SLAB, PART = 384, 3072, 1536, 96
 PLANE = DEPTH // 2
-WIDTHS = (256, 128, 128, 128, 128)
+WIDTHS = (128, 256, 128, 128, 128)
 NCH = len(WIDTHS)
 FROM = [2 * sum(WIDTHS[:j]) for j in range(NCH)]
 ORDER = (
-    ("hop", 0), ("ag0", 0, 0), ("ag0", 0, 1), ("ag0", 1, 0), ("ag0", 1, 1), ("ag0", 2, 1), ("agx", 0, 0), ("ag0", 2, 0),
-    ("agx", 0, 1), ("hop", 1), ("ag0", 3, 0), ("ag0", 3, 1), ("ag0", 4, 0), ("hop", 2), ("ag1", 0, 0), ("hop", 3),
-    ("hop", 4), ("ag0", 4, 1), ("ag1", 0, 1), ("agx", 1, 0), ("agx", 2, 0), ("agx", 1, 1), ("exchange", 0),
-    ("agx", 2, 1), ("agx", 3, 0), ("ag2", 0, 0), ("ag1", 1, 0), ("agx", 4, 0), ("ag2", 0, 1), ("prepare", 0),
-    ("prepare", 1), ("prepare", 2), ("prepare", 3), ("ag1", 2, 1), ("ag1", 2, 0), ("ag1", 1, 1), ("agx", 3, 1),
-    ("agx", 4, 1), ("exchange", 1), ("ag3", 0, 0), ("ag1", 3, 0), ("exchange", 2), ("ag1", 4, 0), ("ag3", 0, 1),
-    ("ag2", 1, 0), ("exchange", 3), ("ag1", 3, 1), ("ag2", 1, 1), ("prepare", 4), ("prepare", 5), ("ag4", 0, 1),
-    ("ag2", 2, 0), ("product1", 0, 1), ("ag2", 2, 1), ("sum1", 0, 1), ("ag4", 0, 0), ("ag3", 1, 1), ("ag1", 4, 1),
-    ("ag3", 1, 0), ("product1", 0, 0), ("sum1", 0, 0), ("ag3", 2, 1), ("ag3", 2, 0), ("ag2", 3, 1), ("ag4", 1, 1),
-    ("ag2", 4, 1), ("ag2", 3, 0), ("ag4", 1, 0), ("ag2", 4, 0), ("take", 0), ("take", 1), ("take", 2), ("take", 3),
-    ("sum2", 0, 1), ("ag4", 2, 1), ("product1", 1, 0), ("sum2", 0, 0), ("ag4", 2, 0), ("product1", 2, 0),
-    ("sum3", 0, 1), ("sum1", 1, 0), ("ag3", 3, 0), ("ag3", 3, 1), ("sum1", 2, 0), ("sum3", 0, 0), ("product2", 0, 1),
-    ("product2", 0, 0), ("ag3", 4, 1), ("sum2", 1, 0), ("ag3", 4, 0), ("rs0", 0, 1), ("sum2", 2, 0), ("rs0", 0, 0),
-    ("ag4", 3, 1), ("ag4", 3, 0), ("product1", 3, 0), ("sum3", 1, 0), ("ag4", 4, 1), ("ag4", 4, 0), ("sum1", 3, 0),
-    ("product1", 4, 0), ("sum3", 2, 0), ("rs1", 0, 1), ("rs1", 0, 0), ("sum1", 4, 0), ("product2", 1, 0),
-    ("sum2", 3, 0), ("rs0", 1, 1), ("rs0", 1, 0), ("product2", 2, 0), ("rs0", 2, 1), ("sum2", 4, 0), ("rs0", 2, 0),
-    ("rs2", 0, 0), ("rs1", 1, 0), ("sum3", 3, 0), ("rs1", 1, 1), ("rs2", 0, 1), ("product2", 3, 0), ("rs0", 3, 1),
-    ("rs0", 3, 0), ("sum3", 4, 0), ("rs1", 2, 1), ("rs1", 2, 0), ("product2", 4, 0), ("rs0", 4, 1), ("rs0", 4, 0),
-    ("rs1", 3, 1), ("rs1", 3, 0), ("rs1", 4, 1), ("rs2", 1, 0), ("rs1", 4, 0), ("rs2", 2, 0), ("rs2", 2, 1),
-    ("rs3", 0, 0), ("rs2", 1, 1), ("rs2", 3, 1), ("rs2", 3, 0), ("rs3", 0, 1), ("rs2", 4, 1), ("rs2", 4, 0),
-    ("rs3", 1, 0), ("rs3", 2, 0), ("rs3", 2, 1), ("rs3", 1, 1), ("rs3", 3, 1), ("rs3", 3, 0), ("rs4", 0, 1),
-    ("rs3", 4, 0), ("rs3", 4, 1), ("rs4", 0, 0), ("rs4", 2, 1), ("rs4", 2, 0), ("rs4", 1, 0), ("rs4", 3, 0),
-    ("rs4", 1, 1), ("rs4", 3, 1), ("rs4", 4, 0), ("rs4", 4, 1),
+    ("hop", 0), ("ag0", 0, 0), ("ag0", 0, 1), ("ag0", 1, 0), ("ag0", 1, 1), ("agx", 0, 0), ("ag0", 2, 1), ("ag0", 2, 0),
+    ("agx", 0, 1), ("hop", 1), ("hop", 2), ("ag0", 3, 1), ("ag0", 3, 0), ("ag0", 4, 1), ("ag1", 0, 0), ("ag0", 4, 0),
+    ("hop", 3), ("ag1", 0, 1), ("hop", 4), ("agx", 1, 0), ("exchange", 0), ("ag2", 0, 0), ("ag2", 0, 1), ("ag1", 1, 0),
+    ("exchange", 1), ("agx", 1, 1), ("agx", 3, 1), ("agx", 4, 0), ("agx", 3, 0), ("agx", 4, 1), ("agx", 2, 1),
+    ("ag3", 0, 1), ("ag1", 1, 1), ("ag3", 0, 0), ("agx", 2, 0), ("exchange", 2), ("ag2", 1, 0), ("ag2", 1, 1),
+    ("prepare", 0), ("prepare", 1), ("prepare", 2), ("prepare", 3), ("ag1", 3, 1), ("ag1", 2, 0), ("ag1", 3, 0),
+    ("ag4", 0, 1), ("ag4", 0, 0), ("ag1", 4, 1), ("ag1", 4, 0), ("ag1", 2, 1), ("product1", 0, 0), ("prepare", 4),
+    ("prepare", 5), ("sum1", 0, 0), ("ag3", 1, 1), ("exchange", 3), ("ag3", 1, 0), ("ag2", 2, 0), ("ag2", 2, 1),
+    ("sum2", 0, 0), ("ag4", 1, 1), ("ag2", 3, 0), ("ag4", 1, 0), ("product1", 1, 1), ("ag2", 3, 1), ("product1", 1, 0),
+    ("sum1", 1, 1), ("take", 0), ("take", 1), ("take", 2), ("take", 3), ("ag3", 2, 1), ("ag3", 2, 0), ("sum3", 0, 0),
+    ("sum1", 1, 0), ("ag3", 3, 1), ("ag2", 4, 1), ("ag3", 3, 0), ("product2", 0, 0), ("sum2", 1, 1), ("ag4", 2, 0),
+    ("ag2", 4, 0), ("ag4", 2, 1), ("product1", 2, 0), ("ag4", 3, 1), ("sum2", 1, 0), ("rs0", 0, 0), ("ag4", 3, 0),
+    ("rs0", 0, 1), ("sum1", 2, 0), ("sum3", 1, 1), ("product1", 3, 0), ("product2", 1, 1), ("sum3", 1, 0),
+    ("sum1", 3, 0), ("ag3", 4, 1), ("ag3", 4, 0), ("rs0", 1, 1), ("product2", 1, 0), ("sum2", 2, 0), ("rs0", 1, 0),
+    ("sum2", 3, 0), ("ag4", 4, 1), ("ag4", 4, 0), ("product1", 4, 0), ("rs1", 0, 0), ("sum3", 2, 0), ("rs1", 1, 1),
+    ("sum1", 4, 0), ("rs1", 0, 1), ("rs1", 1, 0), ("product2", 2, 0), ("sum3", 3, 0), ("rs0", 2, 0), ("rs0", 2, 1),
+    ("sum2", 4, 0), ("product2", 3, 0), ("rs0", 3, 1), ("rs2", 1, 1), ("rs1", 2, 1), ("rs0", 3, 0), ("sum3", 4, 0),
+    ("rs2", 1, 0), ("rs1", 2, 0), ("rs1", 3, 1), ("product2", 4, 0), ("rs0", 4, 0), ("rs0", 4, 1), ("rs1", 3, 0),
+    ("rs2", 2, 0), ("rs2", 0, 0), ("rs1", 4, 0), ("rs2", 0, 1), ("rs1", 4, 1), ("rs2", 2, 1), ("rs2", 3, 1),
+    ("rs3", 2, 0), ("rs2", 3, 0), ("rs3", 1, 1), ("rs3", 0, 0), ("rs2", 4, 0), ("rs2", 4, 1), ("rs3", 1, 0),
+    ("rs3", 2, 1), ("rs3", 3, 0), ("rs3", 3, 1), ("rs4", 0, 0), ("rs3", 0, 1), ("rs4", 1, 1), ("rs3", 4, 0),
+    ("rs3", 4, 1), ("rs4", 2, 1), ("rs4", 1, 0), ("rs4", 2, 0), ("rs4", 3, 0), ("rs4", 3, 1), ("rs4", 0, 1),
+    ("rs4", 4, 0), ("rs4", 4, 1),
 )
 MESH = pl.DeviceIdType.MESH
 F32, BF16 = jnp.float32, jnp.bfloat16

time: 160 us -> 160 us (level)
  no operation moved by 1% of the time
where the time goes in v6:
time: 160 us; the launch traced here: 159 us
  Pallas kernels  157 us (98%)
  local copies, waits for them, and re-layouts  1.92 us (1%)
    pallas_call x1, Pallas kernels, per_device(): pl.pallas_call(kernel, out_shape=jax.ShapeDtypeStruct((PART, SLAB), F32),...  157 us

profile of v6, /device:TPU:1, one launch (start us, length us, event | category | flops | bytes accessed | tf_op | source)
XLA Modules:
  0.0 158.9 jit_solution(4826838170201849928)
XLA Ops:
  0.0 157.0 %rebase.1 = f32[96,1536]{1,0:T(8,128)} custom-call(f32[384,3072]{1,0:T(8,128)} %q_hbm.1, f32[384,3072]{1,0:T(8,128)} %u_hbm.1, f32[96,1536]{1,0:T(8,128)} %m_hbm.1), custom_call_target="tpu_custom_call" | custom-call | flops 21699999744 | bytes 10000000 | tf_op jit(solution)/shard_map/rebase/pallas_call | solution.py:360
  157.0 1.9 %copy.5 = f32[96,1536]{1,0:T(8,128)} copy(f32[96,1536]{1,0:T(8,128)} %rebase.1) | data formatting | bytes 1179648

commit v7 on v6

--- a/solution.py
+++ b/solution.py
@@ -266,7 +266,7 @@
             for i in range(10):
                 sent(("ag", j, h, i))
 
-        @pl.loop(0, 4)
+        @pl.loop(0, 4, unroll=True)
         def _(i):
             at = pl.ds(pl.multiple_of(i * 192, 192), 192)
             for n, h in enumerate(hs):
@@ -274,7 +274,7 @@
                 shl[0, at, pl.ds(n * w, w)] = hi
                 shl[1, at, pl.ds(n * w, w)] = lo
 
-        @pl.loop(0, 4)
+        @pl.loop(0, 4, unroll=True)
         def _(seg):
             both = jnp.dot(uts[seg], shl[0, :, pl.ds(0, len(hs) * w)], preferred_element_type=F32)
             rest = jnp.dot(uts[seg, pl.ds(0, 384), :], shl[1, :, pl.ds(0, len(hs) * w)], preferred_element_type=F32)

time: 160 us -> 160 us (level)
  no operation moved by 1% of the time
where the time goes in v7:
time: 160 us; the launch traced here: 159 us
  Pallas kernels  157 us (98%)
  local copies, waits for them, and re-layouts  1.92 us (1%)
    pallas_call x1, Pallas kernels, per_device(): pl.pallas_call(kernel, out_shape=jax.ShapeDtypeStruct((PART, SLAB), F32),...  157 us

profile of v7, /device:TPU:1, one launch (start us, length us, event | category | flops | bytes accessed | tf_op | source)
XLA Modules:
  0.0 158.9 jit_solution(8875960271663138881)
XLA Ops:
  0.0 156.9 %rebase.1 = f32[96,1536]{1,0:T(8,128)} custom-call(f32[384,3072]{1,0:T(8,128)} %q_hbm.1, f32[384,3072]{1,0:T(8,128)} %u_hbm.1, f32[96,1536]{1,0:T(8,128)} %m_hbm.1), custom_call_target="tpu_custom_call" | custom-call | flops 21699999744 | bytes 10000000 | tf_op jit(solution)/shard_map/rebase/pallas_call | solution.py:360
  157.0 1.9 %copy.5 = f32[96,1536]{1,0:T(8,128)} copy(f32[96,1536]{1,0:T(8,128)} %rebase.1) | data formatting | bytes 1179648
